TPU v7x, 128 devices: a whole 4x4x4 slice. The times are simulated.
128 devices in a mesh: ep: 16 (over z_lo, y, core), fsdp: 8 (over x, z_hi).
Axes of the slice: x: 4, y: 4, z: 4 (z_hi: 2, z_lo: 2; z = z_hi * 2 + z_lo), core: 2. Of those that a mesh axis runs over, the one named last changes fastest.
Arguments:
- moe_input: bfloat16 [4608, 7168], P(('ep', 'fsdp')), may hold values from -6 to 6
- out_grad: bfloat16 [4608, 7168], P(('ep', 'fsdp')), may hold values from -6 to 6
- expert_ids: int32 [4608, 1], P(('ep', 'fsdp')), may hold values from 0 to 15; in each aligned block of 36 rows (0 to 35, 36 to 71, ...) at most 7 rows name the same one
- gate_values: bfloat16 [4608, 1], P(('ep', 'fsdp')), may hold values from 0.19921875 to 1
- w_gate: bfloat16 [16, 7168, 2048], P('ep', None, 'fsdp'), may hold values from -0.0625 to 0.0625
- w_up: bfloat16 [16, 7168, 2048], P('ep', None, 'fsdp'), may hold values from -0.0625 to 0.0625
- w_down: bfloat16 [16, 2048, 7168], P('ep', 'fsdp'), may hold values from -0.125 to 0.125
Outputs:
- moe_grad: bfloat16 [4608, 7168], P(('ep', 'fsdp'))
- gate_grad: bfloat16 [4608, 1], P(('ep', 'fsdp'))
- grad_w_gate: bfloat16 [16, 7168, 2048], P('ep', None, 'fsdp')
- grad_w_up: bfloat16 [16, 7168, 2048], P('ep', None, 'fsdp')
- grad_w_down: bfloat16 [16, 2048, 7168], P('ep', 'fsdp')
Inputs may be any that keep to these rules, and one draw needn't show every extreme that they name: `expert_ids`: in each aligned block of 36 rows (the rows of one device) no expert is named by more than 7 routes, and in every draw some block names one expert exactly 7 times.
All inputs are finite; a program needn't handle non-finite values.
Results may differ from a plain program's by a relative error of at most 0.022.
Values may be sent and summed in bfloat16 or wider, within the bound.
A program may use at most 192 MiB of HBM per device.

v0:
```python
import math

import jax
import jax.numpy as jnp
from jax import lax
from jax.sharding import PartitionSpec as P


def silu_parts(value):
    sig = jax.nn.sigmoid(value)
    return (value * sig, sig * (1.0 + value * (1.0 - sig)))


def contract_rows(left, right):
    return lax.dot_general(
        left, right, (((0,), (0,)), ((), ())), preferred_element_type=jnp.float32
    )


def contract_cols(left, right):
    return lax.dot_general(
        left, right, (((1,), (1,)), ((), ())), preferred_element_type=jnp.float32
    )


def body(moe_input, out_grad, expert_ids, gate_values, w_gate, w_up, w_down):
    tok_rows = moe_input.shape[0]
    width = moe_input.shape[1]
    topw = expert_ids.shape[1]
    experts = lax.axis_size("ep")
    groups = lax.axis_size("fsdp")
    capacity = (3 * tok_rows * topw + experts - 1) // experts
    routes = tok_rows * topw
    flat_ids = expert_ids.reshape(routes)
    onehot = (flat_ids[:, None] == jnp.arange(experts, dtype=jnp.int32)[None, :]).astype(jnp.int32)
    earlier = jnp.cumsum(onehot, axis=0) - onehot
    slot_index = jnp.sum(earlier * onehot, axis=1)
    target = flat_ids * capacity + slot_index
    placing = (jnp.arange(experts * capacity, dtype=jnp.int32)[:, None] == target[None, :]).astype(
        jnp.bfloat16
    )
    route_input = jnp.repeat(moe_input, topw, axis=0)
    route_grad = jnp.repeat(out_grad, topw, axis=0)
    send_input = (
        jnp.dot(placing, route_input, preferred_element_type=jnp.float32)
        .astype(jnp.bfloat16)
        .reshape(experts, capacity, width)
    )
    send_grad = (
        jnp.dot(placing, route_grad, preferred_element_type=jnp.float32)
        .astype(jnp.bfloat16)
        .reshape(experts, capacity, width)
    )
    send_gate = jnp.sum(
        placing.astype(jnp.float32) * gate_values.reshape(1, routes).astype(jnp.float32), axis=1
    )
    send_gate = send_gate.astype(jnp.bfloat16).reshape(experts, capacity)
    recv_input, recv_grad, recv_gate = (
        lax.all_to_all(send_input, "ep", split_axis=0, concat_axis=0, tiled=True),
        lax.all_to_all(send_grad, "ep", split_axis=0, concat_axis=0, tiled=True),
        lax.all_to_all(send_gate, "ep", split_axis=0, concat_axis=0, tiled=True),
    )
    weight_gate = w_gate[0]
    weight_up = w_up[0]
    weight_down = w_down[0]
    expert_scale = 1.0 / math.sqrt(tok_rows * groups)
    gate_scale = 1.0 / math.sqrt(width)
    piece_input = lax.all_gather(recv_input, "fsdp", axis=0, tiled=True)
    piece_grad = lax.all_gather(recv_grad, "fsdp", axis=0, tiled=True)
    piece_gate = lax.all_gather(recv_gate, "fsdp", axis=0, tiled=True)
    count = piece_input.shape[0] * piece_input.shape[1]
    rows_in = piece_input.reshape(count, width)
    rows_grad = piece_grad.reshape(count, width)
    gates = piece_gate.reshape(count, 1).astype(jnp.float32)
    pre_gate = jnp.dot(rows_in, weight_gate, preferred_element_type=jnp.float32)
    pre_up = jnp.dot(rows_in, weight_up, preferred_element_type=jnp.float32)
    act, slope = silu_parts(pre_gate)
    hidden = (act * pre_up).astype(jnp.bfloat16)
    raw = contract_cols(rows_grad, weight_down)
    scaled = gates * raw
    grad_pre_gate = (scaled * pre_up * slope).astype(jnp.bfloat16)
    grad_pre_up = (scaled * act).astype(jnp.bfloat16)
    gated_grad = (gates * rows_grad.astype(jnp.float32)).astype(jnp.bfloat16)
    acc_gate = contract_rows(rows_in, grad_pre_gate)
    acc_up = contract_rows(rows_in, grad_pre_up)
    acc_down = contract_rows(hidden, gated_grad)
    rows_back = contract_cols(grad_pre_gate, weight_gate) + contract_cols(grad_pre_up, weight_up)
    gate_back = jnp.sum(hidden.astype(jnp.float32) * raw, axis=1) * gate_scale
    part_rows = rows_back
    part_gate = gate_back
    acc_gate, acc_up, acc_down, part_rows, part_gate = (
        acc_gate,
        acc_up,
        acc_down,
        part_rows,
        part_gate,
    )
    grad_w_gate = (acc_gate * expert_scale).astype(jnp.bfloat16)[None]
    grad_w_up = (acc_up * expert_scale).astype(jnp.bfloat16)[None]
    grad_w_down = (acc_down * expert_scale).astype(jnp.bfloat16)[None]
    summed_rows, summed_gate = (
        lax.psum_scatter(
            part_rows.astype(jnp.bfloat16), "fsdp", scatter_dimension=0, tiled=True
        ).astype(jnp.float32),
        lax.psum_scatter(
            part_gate.astype(jnp.bfloat16), "fsdp", scatter_dimension=0, tiled=True
        ).astype(jnp.float32),
    )
    back_rows = summed_rows.astype(jnp.bfloat16).reshape(experts, capacity, width)
    back_gate = summed_gate.astype(jnp.bfloat16).reshape(experts, capacity)
    ret_rows, ret_gate = (
        lax.all_to_all(back_rows, "ep", split_axis=0, concat_axis=0, tiled=True),
        lax.all_to_all(back_gate, "ep", split_axis=0, concat_axis=0, tiled=True),
    )
    flat_rows = ret_rows.reshape(experts * capacity, width)
    route_back = contract_rows(placing, flat_rows)
    moe_grad = jnp.sum(route_back.reshape(tok_rows, topw, width), axis=1).astype(jnp.bfloat16)
    gate_back = jnp.sum(
        placing.astype(jnp.float32) * ret_gate.reshape(experts * capacity, 1).astype(jnp.float32),
        axis=0,
    )
    gate_grad = gate_back.reshape(tok_rows, topw).astype(jnp.bfloat16)
    return (moe_grad, gate_grad, grad_w_gate, grad_w_up, grad_w_down)


def solution(mesh):
    placed = (
        P(("ep", "fsdp"), None),
        P(("ep", "fsdp"), None),
        P(("ep", "fsdp"), None),
        P(("ep", "fsdp"), None),
        P("ep", None, "fsdp"),
        P("ep", None, "fsdp"),
        P("ep", "fsdp", None),
    )
    return jax.shard_map(
        body,
        mesh=mesh,
        in_specs=placed,
        out_specs=(
            P(("ep", "fsdp"), None),
            P(("ep", "fsdp"), None),
            P("ep", None, "fsdp"),
            P("ep", None, "fsdp"),
            P("ep", "fsdp", None),
        ),
        check_vma=False,
    )
```

profile of v0, /device:TPU:41, one launch (start us, length us, event | category | flops | bytes accessed | tf_op | source)
XLA Modules:
  0.0 725.2 jit_solution(5310549208032114332)
XLA Ops:
  7.2 0.0 all-gather.4.cloned.1.call-start
  7.2 0.8 fusion.21
  8.0 0.1 reduce_window_sum.11
  8.1 0.8 select_reduce_fusion
  8.9 0.7 multiply_add_fusion
  9.6 1.8 convolution_convert_fusion.1
  11.5 1.8 reshape.103
  13.2 28.4 %all_to_all.34 = bf16[16,7,7168]{2,1,0:T(8,128)(2,1)S(1)} all-to-all(bf16[16,7,7168]{2,1,0:T(8,128)(2,1)S(1)} %reshape.103), channel_id=1, replica_groups=mesh['ep'=16,'fsdp'=8] {'ep'}, dimensions={0} | all-to-all | bytes 3211264 | tf_op jit(solution)/shard_map/all_to_all | solution.py:60
  41.6 2.2 copy.25
  43.8 0.0 all-gather.6.cloned.1.call-start
  43.9 1.9 convolution_convert_fusion
  45.7 1.8 reshape.105
  47.5 30.8 %all_to_all.35 = bf16[16,7,7168]{2,1,0:T(8,128)(2,1)S(1)} all-to-all(bf16[16,7,7168]{2,1,0:T(8,128)(2,1)S(1)} %reshape.105), channel_id=1, replica_groups=mesh['ep'=16,'fsdp'=8] {'ep'}, dimensions={0} | all-to-all | bytes 3211264 | tf_op jit(solution)/shard_map/all_to_all | solution.py:59
  78.3 2.2 copy.27
  80.5 0.6 dynamic-slice
  81.8 127.8 %all-gather.4.cloned.1.call-done = bf16[128,7,7168]{2,0,1:T(8,128)(2,1)} async-done(((bf16[16,7,7168]{2,0,1:T(8,128)(2,1)}), bf16[128,7,7168]{2,0,1:T(8,128)(2,1)}) %all-gather.4.cloned.1.call-update) | async-done | bytes 12845072 | tf_op jit(solution)/shard_map/all_gather | solution.py:69
  209.6 16.0 %copy.26 = bf16[128,7,7168]{2,1,0:T(8,128)(2,1)} copy(bf16[128,7,7168]{2,0,1:T(8,128)(2,1)} %all-gather.4.cloned.1.call-done) | data formatting | bytes 25690112 | tf_op jit(solution)/shard_map/all_gather | solution.py:69
  225.6 17.4 %reshape.104 = bf16[896,7168]{1,0:T(8,128)(2,1)} reshape(bf16[128,7,7168]{2,1,0:T(8,128)(2,1)} %copy.26) | data formatting | bytes 25690112 | tf_op jit(solution)/shard_map/reshape | solution.py:73
  243.0 117.1 %all-gather.6.cloned.1.call-done = bf16[128,7,7168]{2,0,1:T(8,128)(2,1)} async-done(((bf16[16,7,7168]{2,0,1:T(8,128)(2,1)}), bf16[128,7,7168]{2,0,1:T(8,128)(2,1)}) %all-gather.6.cloned.1.call-update) | async-done | bytes 12845072 | tf_op jit(solution)/shard_map/all_gather | solution.py:68
  360.0 15.8 %copy.28 = bf16[128,7,7168]{2,1,0:T(8,128)(2,1)} copy(bf16[128,7,7168]{2,0,1:T(8,128)(2,1)} %all-gather.6.cloned.1.call-done) | data formatting | bytes 25690112 | tf_op jit(solution)/shard_map/all_gather | solution.py:68
  375.8 17.4 %reshape.106 = bf16[896,7168]{1,0:T(8,128)(2,1)} reshape(bf16[128,7,7168]{2,1,0:T(8,128)(2,1)} %copy.28) | data formatting | bytes 25690112 | tf_op jit(solution)/shard_map/reshape | solution.py:72
  393.2 9.1 %fusion.11 = f32[896,256]{0,1:T(8,128)S(1)} fusion(bf16[896,7168]{1,0:T(8,128)(2,1)} %reshape.106, bf16[1,7168,256]{2,1,0:T(8,128)(2,1)} %param.11), kind=kOutput, calls=%fused_computation.18 | convolution fusion | flops 3288334336 | bytes 17432576 | tf_op jit(solution)/shard_map/dot_general | solution.py:75
  402.3 7.4 %fusion.14 = f32[896,256]{0,1:T(8,128)S(1)} fusion(bf16[896,7168]{1,0:T(8,128)(2,1)} %reshape.106, bf16[1,7168,256]{2,1,0:T(8,128)(2,1)S(1)} %copy-done.2), kind=kOutput, calls=%fused_computation.21 | convolution fusion | flops 3288334336 | bytes 17432576 | tf_op jit(solution)/shard_map/dot_general | solution.py:76
  409.7 11.1 %multiply_reduce_fusion = (f32[896]{0:T(1024)S(1)}, bf16[896,256]{0,1:T(8,128)(2,1)}, f32[896,256]{0,1:T(8,128)}) fusion(f32[896,256]{0,1:T(8,128)S(1)} %fusion.14, f32[896,256]{0,1:T(8,128)S(1)} %fusion.11, bf16[896,7168]{1,0:T(8,128)(2,1)} %reshape.104, bf16[1,256,7168]{2,1,0:T(8,128)(2,1)} %param.13), kind=kOutput, calls=%fused_computation.25 | convolution fusion | flops 3290397696 | bytes 19729920 | tf_op jit(solution)/shard_map/dot_general | solution.py:21
  420.8 16.8 %all-reduce = bf16[896]{0:T(1024)(128)(2,1)S(1)} all-reduce(bf16[896]{0:T(1024)(128)(2,1)S(1)} %multiply_convert_fusion.11), channel_id=4, replica_groups=mesh['ep'=16,'fsdp'=8] {'fsdp'}, use_global_device_ids=true, to_apply=%region_5.6.clone | all-reduce | flops 896 | bytes 3584
  437.6 0.1 dynamic-slice.1
  437.7 0.7 all_to_all.28
  438.4 10.2 %all-to-all-start.4 = ((bf16[16,1,7]{2,1,0:T(2,128)(2,1)}), bf16[16,1,7]{2,1,0:T(2,128)(2,1)S(1)}, u32[]{:S(2)}, u32[]{:S(2)}) async-start(bf16[16,1,7]{2,1,0:T(2,128)(2,1)} %all_to_all.28), calls=%async_computation.5 | async-start | bytes 16384 | tf_op jit(solution)/shard_map/all_to_all | solution.py:113
  448.7 3.3 all-to-all-done.4
  452.0 0.1 reshape.111
  452.1 0.7 fusion.20
  452.8 0.1 convert_element_type.148
  452.9 8.6 %all_to_all.36 = bf16[16,1,7]{2,1,0:T(2,128)(2,1)S(1)} all-to-all(bf16[16,1,7]{2,1,0:T(2,128)(2,1)S(1)} %convert_element_type.148), channel_id=1, replica_groups=mesh['ep'=16,'fsdp'=8] {'ep'}, dimensions={0} | all-to-all | bytes 448 | tf_op jit(solution)/shard_map/all_to_all | solution.py:61
  461.5 27.8 %all-gather = bf16[128,1,7]{2,1,0:T(2,128)(2,1)S(1)} all-gather(bf16[16,1,7]{2,1,0:T(2,128)(2,1)S(1)} %all_to_all.36), channel_id=2, replica_groups=mesh['ep'=16,'fsdp'=8] {'fsdp'}, dimensions={0}, use_global_device_ids=true | all-gather | bytes 2016 | tf_op jit(solution)/shard_map/all_gather | solution.py:70
  489.3 0.2 convert_reduce_fusion
  489.5 0.2 reshape.110
  489.7 1.9 multiply_convert_fusion.9
  491.7 14.1 %fusion.9 = f32[896,7168]{1,0:T(8,128)} fusion(bf16[896,256]{0,1:T(8,128)(2,1)S(1)} %get-tuple-element.10, bf16[1,7168,256]{2,1,0:T(8,128)(2,1)} %param.11), kind=kOutput, calls=%fused_computation.16 | convolution fusion | flops 3288334336 | bytes 29818880 | tf_op jit(solution)/shard_map/dot_general | solution.py:21
  505.8 16.9 %add_convert_fusion = bf16[896,7168]{1,0:T(8,128)(2,1)} fusion(f32[896,7168]{1,0:T(8,128)} %fusion.9, bf16[896,256]{0,1:T(8,128)(2,1)S(1)} %get-tuple-element.9, bf16[1,7168,256]{2,1,0:T(8,128)(2,1)} %param.12), kind=kOutput, calls=%fused_computation.1 | convolution fusion | flops 3301179392 | bytes 42663936 | tf_op jit(solution)/shard_map/dot_general | solution.py:21
  522.7 10.6 %fusion.7 = bf16[1,7168,256]{2,1,0:T(8,128)(2,1)} fusion(bf16[896,7168]{1,0:T(8,128)(2,1)} %reshape.106, bf16[896,256]{0,1:T(8,128)(2,1)S(1)} %get-tuple-element.9), kind=kOutput, calls=%fused_computation.11 | convolution fusion | flops 3292004352 | bytes 16973824 | tf_op jit(solution)/shard_map/dot_general | solution.py:15
  533.3 147.1 %reduce-scatter.2.cloned.1.call-done = bf16[112,7168]{1,0:T(8,128)(2,1)} async-done(((bf16[896,7168]{1,0:T(8,128)(2,1)}), bf16[112,7168]{1,0:T(8,128)(2,1)}) %reduce-scatter.2.cloned.1.call-update) | async-done | bytes 1605648 | tf_op jit(solution)/shard_map/reduce_scatter | solution.py:102
  680.4 2.7 reshape.107
  683.1 7.0 all-to-all-start.3
  690.1 10.9 %fusion.6 = bf16[1,256,7168]{2,1,0:T(8,128)(2,1)} fusion(bf16[896,256]{0,1:T(8,128)(2,1)} %get-tuple-element.8, bf16[896,7168]{1,0:T(8,128)(2,1)} %reshape.104, f32[896]{0:T(1024)S(1)} %reshape.110), kind=kOutput, calls=%fused_computation.10 | convolution fusion | flops 3311271936 | bytes 16977408 | tf_op jit(solution)/shard_map/dot_general | solution.py:15
  701.1 5.6 fusion.8
  706.7 7.6 %all-to-all-done.3 = bf16[16,7,7168]{2,1,0:T(8,128)(2,1)S(1)} async-done(((bf16[16,7,7168]{2,1,0:T(8,128)(2,1)}), bf16[16,7,7168]{2,1,0:T(8,128)(2,1)S(1)}, u32[]{:S(2)}, u32[]{:S(2)}) %all-to-all-start.3) | async-done | bytes 1605664 | tf_op jit(solution)/shard_map/all_to_all | solution.py:112
  714.3 1.5 reshape.108
  715.8 2.6 convolution_convert_fusion.2
  (30 shorter events, 0.2 us)
Async XLA Ops:
  7.2 2.5 copy-start
  7.2 36.7 %copy-start.4 = (bf16[36,7168]{1,0:T(8,128)(2,1)S(1)}, bf16[36,7168]{1,0:T(8,128)(2,1)}, u32[]{:S(2)}) copy-start(bf16[36,7168]{1,0:T(8,128)(2,1)} %param.7) | copy-start | bytes 1548292
  7.2 202.4 %all-gather.4.cloned.1.call-start = ((), (), s32[]{:S(2)}) async-start(), calls=%async_computation.6 | async-start | bytes 14450688 | tf_op jit(solution)/shard_map/all_gather | solution.py:69
  43.8 36.7 %copy-start.6 = (u32[128]{0:T(128)S(1)}, u32[128]{0:T(128)}, u32[]{:S(2)}) copy-start(u32[128]{0:T(128)} %constant.26) | copy-start | bytes 1540
  43.8 316.2 %all-gather.6.cloned.1.call-start = ((), (), s32[]{:S(2)}) async-start(), calls=%async_computation.7 | async-start | bytes 14450688 | tf_op jit(solution)/shard_map/all_gather | solution.py:68
  393.2 9.1 %copy-start.2 = (bf16[1,7168,256]{2,1,0:T(8,128)(2,1)S(1)}, bf16[1,7168,256]{2,1,0:T(8,128)(2,1)}, u32[]{:S(2)}) copy-start(bf16[1,7168,256]{2,1,0:T(8,128)(2,1)} %param.12) | copy-start | bytes 11010052
  409.6 11.2 %copy-start.3 = (f32[896,256]{0,1:T(8,128)}, f32[896,256]{0,1:T(8,128)S(1)}, u32[]{:S(2)}) copy-start(f32[896,256]{0,1:T(8,128)S(1)} %fusion.14) | copy-start | bytes 2752516
  409.7 39.0 %copy-start.5 = (bf16[36,1]{0,1:T(2,128)(2,1)S(1)}, bf16[36,1]{0,1:T(2,128)(2,1)}, u32[]{:S(2)}) copy-start(bf16[36,1]{0,1:T(2,128)(2,1)} %param.10) | copy-start | bytes 220
  438.4 13.6 %all-to-all-start.4 = ((bf16[16,1,7]{2,1,0:T(2,128)(2,1)}), bf16[16,1,7]{2,1,0:T(2,128)(2,1)S(1)}, u32[]{:S(2)}, u32[]{:S(2)}) async-start(bf16[16,1,7]{2,1,0:T(2,128)(2,1)} %all_to_all.28), calls=%async_computation.5 | async-start | bytes 16384 | tf_op jit(solution)/shard_map/all_to_all | solution.py:113
  448.6 231.8 %reduce-scatter.2.cloned.1.call-start = ((), (), s32[]{:S(2)}) async-start(), calls=%async_computation.8 | async-start | bytes 14450688 | tf_op jit(solution)/shard_map/reduce_scatter | solution.py:102
  683.1 17.9 %slice-start = ((s8[12845056]{0:T(1024)(128)(4,1)}), s8[262144]{0:T(1024)(128)(4,1)S(1)}, s32[]{:S(2)}) async-start(s8[12845056]{0:T(1024)(128)(4,1)} %bitcast.43), calls=%async_computation.9 | async-start | bytes 524288
  683.1 31.2 %all-to-all-start.3 = ((bf16[16,7,7168]{2,1,0:T(8,128)(2,1)}), bf16[16,7,7168]{2,1,0:T(8,128)(2,1)S(1)}, u32[]{:S(2)}, u32[]{:S(2)}) async-start(bf16[16,7,7168]{2,1,0:T(8,128)(2,1)} %reshape.107), calls=%async_computation.4 | async-start | bytes 3670016 | tf_op jit(solution)/shard_map/all_to_all | solution.py:112
  690.1 10.9 %slice-start.1 = ((s8[12845056]{0:T(1024)(128)(4,1)}), s8[4194304]{0:T(1024)(128)(4,1)S(1)}, s32[]{:S(2)}) async-start(s8[12845056]{0:T(1024)(128)(4,1)} %bitcast.43), calls=%async_computation.10 | async-start | bytes 8388608
  690.1 10.9 %slice-start.2 = ((s8[12845056]{0:T(1024)(128)(4,1)}), s8[4194304]{0:T(1024)(128)(4,1)S(1)}, s32[]{:S(2)}) async-start(s8[12845056]{0:T(1024)(128)(4,1)} %bitcast.43), calls=%async_computation.11 | async-start | bytes 8388608
  690.1 10.9 %slice-start.3 = ((s8[12845056]{0:T(1024)(128)(4,1)}), s8[4194304]{0:T(1024)(128)(4,1)S(1)}, s32[]{:S(2)}) async-start(s8[12845056]{0:T(1024)(128)(4,1)} %bitcast.43), calls=%async_computation.12 | async-start | bytes 8388608
  701.1 17.4 %copy-start.1 = (bf16[36,7168]{1,0:T(8,128)(2,1)S(1)}, bf16[36,7168]{1,0:T(8,128)(2,1)}, u32[]{:S(2)}) copy-start(bf16[36,7168]{1,0:T(8,128)(2,1)} %param.8) | copy-start | bytes 1548292
Sparse Core Ops, SparseCore 0:
  43.9 165.6 all-gather.3
  212.5 147.5 all-gather.5
  522.8 157.5 reduce-scatter.1
where the time goes:
time: 731 us; the launch traced here: 725 us
  waiting for transfers between devices  403 us (55%)
  blocking collectives  112 us (15%)
  matrix products  92 us (13%)
  local copies, waits for them, and re-layouts  80.4 us (11%)
  starting transfers between devices  17.3 us (2%)
  between operations  14.8 us (2%)
    reduce_scatter x1, waiting for transfers between devices, body(): lax.psum_scatter(part_rows.astype(jnp.bfloat16), 'fsdp', scatter_dimensio...  147 us
    all_gather x1, waiting for transfers between devices, body(): piece_grad = lax.all_gather(recv_grad, 'fsdp', axis=0, tiled=True)  128 us
    all_gather x1, waiting for transfers between devices, body(): piece_input = lax.all_gather(recv_input, 'fsdp', axis=0, tiled=True)  117 us
    dot_general x3, matrix products, contract_cols(): lax.dot_general(left, right, (((1,), (1,)), ((), ())), preferred_element_...  42.1 us
    all_to_all x1, blocking collectives, body(): lax.all_to_all(send_input, 'ep', split_axis=0, concat_axis=0, tiled=True)  30.8 us
    dot_general x4, matrix products, contract_rows(): lax.dot_general(left, right, (((0,), (0,)), ((), ())), preferred_element_...  29.7 us
    all_to_all x1, blocking collectives, body(): lax.all_to_all(send_grad, 'ep', split_axis=0, concat_axis=0, tiled=True)  28.4 us
    all_gather x1, blocking collectives, body(): piece_gate = lax.all_gather(recv_gate, 'fsdp', axis=0, tiled=True)  27.8 us
  transfers between devices with their start and end apart: 5, of which 5 were waited for; matrix products, arithmetic and copies ran while one was open for 9% of the time, Pallas kernels for 0%

commit v1 on v0

v1 whole, which is shorter than its diff:
```python
import functools
import math

import jax
import jax.numpy as jnp
from jax import lax
from jax.experimental import pallas as pl
from jax.experimental.pallas import tpu as pltpu
from jax.sharding import PartitionSpec as P

BF = jnp.bfloat16
F32 = jnp.float32
CAP = 7
UNIT = 16
STEPS = 4
BLOCKS = 8
HALF = BLOCKS * CAP
DENSE = 2 * HALF
CUT = 64
LANES = 128


def nn(left, right):
    return jnp.dot(left, right, preferred_element_type=F32)


def nt(left, right):
    return lax.dot_general(left, right, (((1,), (1,)), ((), ())), preferred_element_type=F32)


def kernel(
    units_hbm, w_gate_hbm, w_up_hbm, w_down_hbm, low_map, high_map, inv_gate,
    moe_grad, gate_grad, grad_gate_hbm, grad_up_hbm, grad_down_hbm, returned_hbm,
    w_gate, w_up, w_down, arrived, chunks, part, far_in, near_in, back, acc, packed, turned,
    w_sem, unit_send, unit_recv, own_send, own_recv, fwd_send, fwd_recv,
    far_send, far_recv, near_send, near_recv, far_free, near_free,
    back_send, back_recv, out_sem,
):
    width = w_gate.shape[0]
    units_of = w_gate.shape[1]
    half_width = width // 2
    ep = lax.axis_index("ep")
    fs = lax.axis_index("fsdp")
    z = lax.rem(fs, 2) * 2 + ep // 8
    y = lax.rem(ep // 2, 4)
    core = lax.rem(ep, 2)
    x = fs // 2

    def at(ax, ay, az, ac):
        return (lax.rem(az, 2) * 8 + ay * 2 + ac, ax * 2 + az // 2)

    def shift(v, n):
        return lax.rem(v + n, 4)

    plus = at(shift(x, 1), y, z, core)
    minus = at(shift(x, 3), y, z, core)
    remote = functools.partial(
        pltpu.make_async_remote_copy, device_id_type=pl.DeviceIdType.MESH
    )

    partners = [plus, minus]
    for dy in range(4):
        for dz in range(4):
            for dc in range(2):
                if dy or dz or dc:
                    partners.append(at(x, shift(y, dy), shift(z, dz), lax.rem(core + dc, 2)))

    weights = [
        pltpu.make_async_copy(w_gate_hbm.at[0], w_gate, w_sem.at[0]),
        pltpu.make_async_copy(w_up_hbm.at[0], w_up, w_sem.at[1]),
        pltpu.make_async_copy(w_down_hbm.at[0], w_down, w_sem.at[2]),
    ]

    barrier = pltpu.get_barrier_semaphore()
    for partner in partners:
        pl.semaphore_signal(barrier, 1, device_id=partner, device_id_type=pl.DeviceIdType.MESH)
    pl.semaphore_wait(barrier, len(partners))

    mine = z * 2 + core
    unit_copies = []
    for k in range(STEPS):
        for dz in range(4):
            for dc in range(2):
                ay, az, ac = shift(y, 4 - k), shift(z, dz), lax.rem(core + dc, 2)
                expert = lax.rem(az, 2) * 8 + ay * 2 + ac
                src = units_hbm.at[expert]
                dst = arrived.at[k * BLOCKS + mine]
                index = (k * 4 + dz) * 2 + dc
                sem = unit_recv.at[k * BLOCKS + mine]
                if k or dz or dc:
                    copy = remote(src, dst, unit_send.at[index], sem, device_id=at(x, ay, az, ac))
                    copy.start()
                    unit_copies.append(copy)
                else:
                    pltpu.make_async_copy(src, dst, sem).start()
    for copy in weights:
        copy.start()

    row = lax.broadcasted_iota(jnp.int32, (DENSE, BLOCKS * UNIT), 0)
    col = lax.broadcasted_iota(jnp.int32, (DENSE, BLOCKS * UNIT), 1)
    upper = (row >= HALF).astype(jnp.int32)
    rest = row - upper * HALF
    block = jnp.zeros_like(row)
    for b in range(1, BLOCKS):
        block = block + (rest >= CAP * b).astype(jnp.int32)
    place = block * UNIT + upper * CAP + (rest - block * CAP)
    select = (col == place).astype(F32).astype(BF)
    row_t = lax.broadcasted_iota(jnp.int32, (BLOCKS * UNIT, DENSE), 1)
    col_t = lax.broadcasted_iota(jnp.int32, (BLOCKS * UNIT, DENSE), 0)
    upper_t = (row_t >= HALF).astype(jnp.int32)
    rest_t = row_t - upper_t * HALF
    block_t = jnp.zeros_like(row_t)
    for b in range(1, BLOCKS):
        block_t = block_t + (rest_t >= CAP * b).astype(jnp.int32)
    place_t = block_t * UNIT + upper_t * CAP + (rest_t - block_t * CAP)
    select_t = (col_t == place_t).astype(F32).astype(BF)

    own = {}
    fwd = {}
    far = {}
    near = {}
    backs = {}

    def take_in(k):
        for b in range(BLOCKS):
            j = k * BLOCKS + b
            pltpu.make_async_copy(arrived.at[j], arrived.at[j], unit_recv.at[j]).wait()
        step = 1024

        def move(i, carry):
            cols = pl.ds(pl.multiple_of(i * step, step), step)
            found = arrived[k * BLOCKS : (k + 1) * BLOCKS, :, cols].reshape(BLOCKS * UNIT, step)
            chunks[k, 0, :, cols] = nn(select, found).astype(BF)
            return carry

        lax.fori_loop(0, width // step, move, 0)
        own[k] = [
            remote(chunks.at[k, 0], chunks.at[k, 1], own_send.at[k, 0], own_recv.at[k, 0], device_id=plus),
            remote(chunks.at[k, 0], chunks.at[k, 2], own_send.at[k, 1], own_recv.at[k, 1], device_id=minus),
        ]
        for copy in own[k]:
            copy.start()

    def forward(k):
        low, high = pl.ds(0, CUT), pl.ds(CUT, DENSE - CUT)
        fwd[k] = [
            remote(chunks.at[k, 1, low], chunks.at[k, 3, low], fwd_send.at[k, 0], fwd_recv.at[k, 0], device_id=plus),
            remote(chunks.at[k, 2, high], chunks.at[k, 3, high], fwd_send.at[k, 1], fwd_recv.at[k, 1], device_id=minus),
        ]
        for i in range(2):
            own[k][i].wait_recv()
            fwd[k][i].start()

    def compute(k):
        for copy in fwd[k]:
            copy.wait_recv()
        rows = 4 * DENSE
        step = 1024
        acc[...] = jnp.zeros_like(acc)

        def gather(i, carry):
            cols = pl.ds(pl.multiple_of(i * step, step), step)
            left = chunks[k, :, :, cols].reshape(rows, step)
            acc[0:rows, 0:units_of] += nn(left, w_gate[cols, :])
            acc[0:rows, units_of : 2 * units_of] += nn(left, w_up[cols, :])
            acc[0:rows, 2 * units_of : 3 * units_of] += nt(left, w_down[:, cols])
            return carry

        lax.fori_loop(0, width // step, gather, 0)
        if k:
            for copy in far[k - 1] + near[k - 1]:
                copy.wait_send()
        blank = jnp.zeros((HALF, units_of), F32)
        for r in range(4):
            ins = pl.ds(r * DENSE, HALF)
            outs = pl.ds(r * DENSE + HALF, HALF)
            pre_gate = acc[ins, 0:units_of]
            pre_up = acc[ins, units_of : 2 * units_of]
            scaled = acc[outs, 2 * units_of : 3 * units_of]
            sig = jax.nn.sigmoid(pre_gate)
            act = pre_gate * sig
            slope = sig * (1.0 + pre_gate * (1.0 - sig))
            hidden = (act * pre_up).astype(BF).astype(F32)
            grad_gate = scaled * pre_up * slope
            grad_up = scaled * act
            piece = jnp.sum(hidden * scaled, axis=1, keepdims=True) * (1.0 / math.sqrt(width))
            acc[ins, 0:units_of] = grad_gate
            acc[ins, units_of : 2 * units_of] = grad_up
            acc[ins, 2 * units_of : 3 * units_of] = blank
            acc[outs, 0:units_of] = blank
            acc[outs, units_of : 2 * units_of] = blank
            acc[outs, 2 * units_of : 3 * units_of] = hidden
            packed[r * HALF : (r + 1) * HALF, 0:units_of] = grad_gate
            packed[r * HALF : (r + 1) * HALF, units_of : 2 * units_of] = grad_up
            part[r, :, half_width : half_width + LANES] = jnp.concatenate(
                [jnp.broadcast_to(piece, (HALF, LANES)), jnp.zeros((HALF, LANES), F32)], axis=0
            ).astype(BF)
        turned[k] = jnp.transpose(acc[...]).astype(BF)
        left_gate = packed[:, 0:units_of].astype(BF)
        left_up = packed[:, units_of : 2 * units_of].astype(BF)
        span = 512

        def rows_back(i, carry):
            lo = pl.ds(pl.multiple_of(i * span, span), span)
            hi = pl.ds(pl.multiple_of(half_width + i * span, span), span)
            r_lo = nt(left_gate, w_gate[lo, :]) + nt(left_up, w_up[lo, :])
            r_hi = nt(left_gate, w_gate[hi, :]) + nt(left_up, w_up[hi, :])
            for r in range(4):
                mine_rows = slice(r * HALF, (r + 1) * HALF)
                part[r, :, lo] = jnp.concatenate([r_lo[mine_rows], r_hi[mine_rows]], axis=0).astype(BF)
            return carry

        lax.fori_loop(0, half_width // span, rows_back, 0)
        if k:
            pl.semaphore_wait(far_free, 2)
        low, high = pl.ds(0, CUT), pl.ds(CUT, DENSE - CUT)
        far[k] = [
            remote(part.at[3, low], far_in.at[0, low], far_send.at[k, 0], far_recv.at[k, 0], device_id=plus),
            remote(part.at[3, high], far_in.at[1, high], far_send.at[k, 1], far_recv.at[k, 1], device_id=minus),
        ]
        for copy in far[k]:
            copy.start()

    def pass_on(k):
        if k:
            pl.semaphore_wait(near_free, 2)
        near[k] = [
            remote(part.at[2], near_in.at[0], near_send.at[k, 0], near_recv.at[k, 0], device_id=plus),
            remote(part.at[1], near_in.at[1], near_send.at[k, 1], near_recv.at[k, 1], device_id=minus),
        ]
        for i, rel, rows, giver in ((0, 2, slice(0, CUT), minus), (1, 1, slice(CUT, DENSE), plus)):
            far[k][i].wait_recv()
            part[rel, rows] = (part[rel, rows].astype(F32) + far_in[i, rows].astype(F32)).astype(BF)
            if k < STEPS - 1:
                pl.semaphore_signal(far_free, 1, device_id=giver, device_id_type=pl.DeviceIdType.MESH)
            near[k][i].start()

    def send_back(k):
        for copy in near[k]:
            copy.wait_recv()
        slot = k % 2
        if k >= 2:
            for copy in backs[k - 2]:
                copy.wait_send()
        full = half_width + LANES
        for first in range(0, full, 1024):
            cols = slice(first, min(first + 1024, full))
            total = nn(select_t, part[0, :, cols]) + nn(select_t, near_in[0, :, cols])
            total = total + nn(select_t, near_in[1, :, cols])
            back[slot, :, :, cols] = total.astype(BF).reshape(BLOCKS, UNIT, cols.stop - cols.start)
        if k < STEPS - 1:
            for giver in (minus, plus):
                pl.semaphore_signal(near_free, 1, device_id=giver, device_id_type=pl.DeviceIdType.MESH)
        me = y * BLOCKS + mine
        backs[k] = []
        for dz in range(4):
            for dc in range(2):
                ay, az, ac = shift(y, k), shift(z, dz), lax.rem(core + dc, 2)
                src = back.at[slot, az * 2 + ac]
                index = (k * 4 + dz) * 2 + dc
                if k or dz or dc:
                    copy = remote(src, returned_hbm.at[me], back_send.at[index], back_recv.at[me], device_id=at(x, ay, az, ac))
                    copy.start()
                    backs[k].append(copy)
                else:
                    kept = pltpu.make_async_copy(src, returned_hbm.at[me], w_sem.at[1])
                    kept.start()
                    kept.wait()

    scale = 1.0 / math.sqrt(36 * 8)
    span = 512
    out_copies = []

    def gradients(first, last):
        def one(i, carry):
            cols = pl.ds(pl.multiple_of(i * span, span), span)
            total = nn(turned[0][:, 0 : 4 * DENSE], chunks[0, :, :, cols].reshape(4 * DENSE, span))
            for k in range(1, STEPS):
                total = total + nn(turned[k][:, 0 : 4 * DENSE], chunks[k, :, :, cols].reshape(4 * DENSE, span))
            total = total * scale
            w_gate[cols, :] = jnp.transpose(total[0:units_of]).astype(BF)
            w_up[cols, :] = jnp.transpose(total[units_of : 2 * units_of]).astype(BF)
            w_down[:, cols] = total[2 * units_of :].astype(BF)
            return carry

        lax.fori_loop(first, last, one, 0)
        rows = pl.ds(first * span, (last - first) * span)
        n = len(out_copies)
        made = [
            pltpu.make_async_copy(w_gate.at[rows], grad_gate_hbm.at[0, rows], out_sem.at[n]),
            pltpu.make_async_copy(w_up.at[rows], grad_up_hbm.at[0, rows], out_sem.at[n + 1]),
            pltpu.make_async_copy(w_down.at[:, rows], grad_down_hbm.at[0, :, rows], out_sem.at[n + 2]),
        ]
        for copy in made:
            copy.start()
        out_copies.extend(made)

    take_in(0)
    take_in(1)
    forward(0)
    take_in(2)
    forward(1)
    take_in(3)
    for copy in weights:
        copy.wait()
    compute(0)
    forward(2)
    pass_on(0)
    send_back(0)
    compute(1)
    forward(3)
    pass_on(1)
    send_back(1)
    compute(2)
    pass_on(2)
    send_back(2)
    compute(3)
    gradients(0, 4)
    pass_on(3)
    gradients(4, 9)
    send_back(3)
    gradients(9, 14)

    for k in range(STEPS):
        for dz in range(4):
            for dc in range(2):
                if k or dz or dc:
                    j = shift(y, 4 - k) * BLOCKS + shift(z, dz) * 2 + lax.rem(core + dc, 2)
                    pltpu.make_async_copy(back.at[0, 0], returned_hbm.at[j], back_recv.at[j]).wait()
    full = half_width + LANES
    pull = pltpu.make_async_copy(returned_hbm, arrived.at[:, :, pl.ds(0, full)], w_sem.at[0])
    pull.start()
    pull.wait()
    for first in range(0, half_width, 512):
        found = arrived[:, :, first : first + 512].reshape(STEPS * BLOCKS * UNIT, 512)
        moe_grad[:, first : first + 512] = nn(low_map[...], found).astype(BF)
        moe_grad[:, half_width + first : half_width + first + 512] = nn(high_map[...], found).astype(BF)
    found = arrived[:, :, half_width:full].reshape(STEPS * BLOCKS * UNIT, LANES)
    gate_grad[...] = (nn(low_map[...], found) * inv_gate[...]).astype(BF)

    for copy in out_copies:
        copy.wait()
    for copy in unit_copies:
        copy.wait_send()
    for k in range(STEPS):
        for copy in own[k] + fwd[k]:
            copy.wait_send()
    for copy in far[STEPS - 1] + near[STEPS - 1] + backs[STEPS - 2] + backs[STEPS - 1]:
        copy.wait_send()


def body(moe_input, out_grad, expert_ids, gate_values, w_gate, w_up, w_down):
    tok_rows, width = moe_input.shape
    hidden = w_gate.shape[2]
    experts = lax.axis_size("ep")
    ids = expert_ids.reshape(tok_rows)
    one_hot = (ids[:, None] == jnp.arange(experts, dtype=jnp.int32)[None, :]).astype(jnp.int32)
    same = (ids[:, None] == ids[None, :]).astype(jnp.int32)
    before = jnp.tril(jnp.ones((tok_rows, tok_rows), jnp.int32), -1)
    slot = jnp.sum(same * before, axis=1)
    gates = gate_values.reshape(tok_rows, 1).astype(F32)
    gated = (gates * out_grad.astype(F32)).astype(BF)
    target = ids * UNIT + slot
    unit_rows = jnp.arange(experts * UNIT, dtype=jnp.int32)[:, None]
    place_x = (unit_rows == target[None, :]).astype(BF)
    place_g = (unit_rows == target[None, :] + CAP).astype(BF)
    units = nn(
        jnp.concatenate([place_x, place_g], axis=1), jnp.concatenate([moe_input, gated], axis=0)
    ).astype(BF).reshape(experts, UNIT, width)
    place = jnp.arange(STEPS * BLOCKS * UNIT, dtype=jnp.int32)
    giver, giver_row = place // UNIT, place % UNIT
    giver_expert = ((giver // 2) % 2) * 8 + (giver // 8) * 2 + giver % 2
    from_expert = giver_expert[None, :] == ids[:, None]
    low_map = (from_expert & (giver_row[None, :] == slot[:, None])).astype(BF)
    high_map = (from_expert & (giver_row[None, :] == slot[:, None] + CAP)).astype(BF)
    inv_gate = jnp.broadcast_to(1.0 / gates, (tok_rows, LANES))
    full = width // 2 + LANES

    vmem = pl.BlockSpec(memory_space=pltpu.VMEM)
    anywhere = pl.BlockSpec(memory_space=pl.ANY)
    dma = pltpu.SemaphoreType.DMA
    grads = pl.pallas_call(
        kernel,
        out_shape=[
            jax.ShapeDtypeStruct((tok_rows, width), BF),
            jax.ShapeDtypeStruct((tok_rows, LANES), BF),
            jax.ShapeDtypeStruct(w_gate.shape, BF),
            jax.ShapeDtypeStruct(w_up.shape, BF),
            jax.ShapeDtypeStruct(w_down.shape, BF),
            jax.ShapeDtypeStruct((STEPS * BLOCKS, UNIT, full), BF),
        ],
        in_specs=[anywhere] * 4 + [vmem] * 3,
        out_specs=[vmem] * 2 + [anywhere] * 4,
        scratch_shapes=[
            pltpu.VMEM((width, hidden), BF),
            pltpu.VMEM((width, hidden), BF),
            pltpu.VMEM((hidden, width), BF),
            pltpu.VMEM((STEPS * BLOCKS, UNIT, width), BF),
            pltpu.VMEM((STEPS, 4, DENSE, width), BF),
            pltpu.VMEM((4, DENSE, full), BF),
            pltpu.VMEM((2, DENSE, full), BF),
            pltpu.VMEM((2, DENSE, full), BF),
            pltpu.VMEM((2, BLOCKS, UNIT, full), BF),
            pltpu.VMEM((512, 3 * hidden), F32),
            pltpu.VMEM((4 * HALF, 2 * hidden), F32),
            pltpu.VMEM((STEPS, 3 * hidden, 512), BF),
            dma((3,)),
            dma((32,)),
            dma((32,)),
            dma((STEPS, 2)),
            dma((STEPS, 2)),
            dma((STEPS, 2)),
            dma((STEPS, 2)),
            dma((STEPS, 2)),
            dma((STEPS, 2)),
            dma((STEPS, 2)),
            dma((STEPS, 2)),
            pltpu.SemaphoreType.REGULAR,
            pltpu.SemaphoreType.REGULAR,
            dma((32,)),
            dma((32,)),
            dma((9,)),
        ],
        compiler_params=pltpu.CompilerParams(
            collective_id=0, has_side_effects=True, vmem_limit_bytes=63 * 2**20
        ),
    )(units, w_gate, w_up, w_down, low_map, high_map, inv_gate)
    moe_grad, gate_wide, grad_gate, grad_up, grad_down, _ = grads
    return (moe_grad, gate_wide[:, 0:1], grad_gate, grad_up, grad_down)


def solution(mesh):
    rows = P(("ep", "fsdp"), None)
    columns = P("ep", None, "fsdp")
    return jax.shard_map(
        body,
        mesh=mesh,
        in_specs=(rows, rows, rows, rows, columns, columns, P("ep", "fsdp", None)),
        out_specs=(rows, rows, columns, columns, P("ep", "fsdp", None)),
        check_vma=False,
    )
```

time: 731 us -> 512 us (0.70)
  Pallas kernels: 0 us -> 487 us
  waiting for transfers between devices: 403 us -> 0 us
  blocking collectives: 112 us -> 0 us
  matrix products: 92 us -> 4.06 us
  local copies, waits for them, and re-layouts: 80.4 us -> 13.3 us
  starting transfers between devices: 17.3 us -> 0 us
  between operations: 14.8 us -> 0.66 us
    pallas_call x0 -> x1, Pallas kernels: none -> 487 us  [body(): pl.pallas_call(kernel, out_shape=[jax.ShapeDtypeStruct((tok_rows, width),...]
    all_gather x2 -> x0, waiting for transfers between devices: 245 us -> none  [the longest x1 128 us: body(): piece_grad = lax.all_gather(recv_grad, 'fsdp', axis=0, tiled=True)]
    reduce_scatter x1 -> x0, waiting for transfers between devices: 147 us -> none  [body(): lax.psum_scatter(part_rows.astype(jnp.bfloat16), 'fsdp', scatter_dimensio...]
    dot_general x11 -> x1, matrix products: 92 us -> 4.06 us  [nn(): return jnp.dot(left, right, preferred_element_type=F32)]
    all_to_all x3 -> x0, blocking collectives: 67.8 us -> none  [the longest x1 30.8 us: body(): lax.all_to_all(send_input, 'ep', split_axis=0, concat_axis=0, tiled=True)]
    reshape x6 -> x0, local copies, waits for them, and re-layouts: 42.5 us -> none  [the longest x1 17.4 us: body(): rows_grad = piece_grad.reshape(count, width)]
    all_gather x2 -> x0, local copies, waits for them, and re-layouts: 31.8 us -> none  [the longest x1 16 us: body(): piece_grad = lax.all_gather(recv_grad, 'fsdp', axis=0, tiled=True)]
    all_gather x1 -> x0, blocking collectives: 27.8 us -> none  [body(): piece_gate = lax.all_gather(recv_gate, 'fsdp', axis=0, tiled=True)]
  transfers between devices with their start and end apart: 5 -> 0, of which waited for: 5 -> 0; matrix products, arithmetic and copies ran while one was open for 9% -> 0% of each run, Pallas kernels for 0% -> 0%
where the time goes in v1:
time: 512 us; the launch traced here: 511 us
  Pallas kernels  487 us (95%)
  local copies, waits for them, and re-layouts  13.3 us (3%)
  other arithmetic  5.57 us (1%)
    pallas_call x1, Pallas kernels, body(): pl.pallas_call(kernel, out_shape=[jax.ShapeDtypeStruct((tok_rows, width),...  487 us
    unnamed x9, local copies, waits for them, and re-layouts  12.7 us

profile of v1, /device:TPU:41, one launch (start us, length us, event | category | flops | bytes accessed | tf_op | source)
XLA Modules:
  0.0 511.0 jit_solution(16134233862950800262)
XLA Ops:
  0.6 0.7 divide_bitcast_fusion
  1.3 0.7 convert_bitcast_fusion
  2.0 0.9 select_reduce_fusion
  2.9 0.7 broadcast_add_fusion.1
  3.6 0.7 broadcast_in_dim.13.inv_gate
  4.3 1.4 fusion.7
  5.7 1.2 multiply_convert_fusion
  6.9 4.1 convolution_convert_fusion
  11.0 487.4 %shard_map.110 = (bf16[36,7168]{1,0:T(8,128)(2,1)}, bf16[36,128]{1,0:T(8,128)(2,1)}, bf16[1,7168,256]{2,1,0:T(8,128)(2,1)}, bf16[1,7168,256]{2,1,0:T(8,128)(2,1)...) custom-call(bf16[16,16,7168]{2,1,0:T(8,128)(2,1)} %bitcast.9, bf16[1,7168,256]{2,1,0:T(8,128)(2,1)} %w_gate_hbm.1, ...), custom_call_target="tpu_custom_call" | custom-call | tf_op jit(solution)/shard_map/pallas_call | solution.py:382
  498.3 1.3 copy.13
  499.6 1.9 copy.22
  501.5 0.0 copy-start.1
  501.5 4.3 copy.23
  505.8 0.0 copy-done.1
  505.8 0.0 copy-start
  505.8 1.9 copy.24
  507.7 1.5 copy-done
  509.2 1.8 copy.25
  (3 shorter events, 0.1 us)
Async XLA Ops:
  501.5 4.3 copy-start.1
  505.8 3.4 copy-start

commit v2 on v0

--- a/solution.py
+++ b/solution.py
@@ -1,9 +1,552 @@
+import functools
 import math
 
 import jax
 import jax.numpy as jnp
 from jax import lax
+from jax.experimental import pallas as pl
+from jax.experimental.pallas import tpu as pltpu
 from jax.sharding import PartitionSpec as P
+
+BF = jnp.bfloat16
+F32 = jnp.float32
+CAP = 7
+UNIT = 16
+FLAG_ROW = 2 * CAP
+STEPS = 4
+BLOCKS = 8
+SLOTS = BLOCKS * UNIT
+LIST = 80
+ROWS = 4 * LIST
+PADDED = 384
+LANES = 128
+MESH = pl.DeviceIdType.MESH
+
+
+def nn(left, right):
+    return jnp.dot(left, right, preferred_element_type=F32)
+
+
+def nt(left, right):
+    return lax.dot_general(left, right, (((1,), (1,)), ((), ())), preferred_element_type=F32)
+
+
+def tn(left, right):
+    return lax.dot_general(left, right, (((0,), (0,)), ((), ())), preferred_element_type=F32)
+
+
+def iota(shape, dim):
+    return lax.broadcasted_iota(jnp.int32, shape, dim)
+
+
+def ones(where):
+    return where.astype(F32).astype(BF)
+
+
+def kernel(
+    moe_input, out_grad, ids_col, ids_row, gates, w_gate_hbm, w_up_hbm, w_down_hbm,
+    moe_grad, gate_grad, overflow, grad_gate_hbm, grad_up_hbm, grad_down_hbm, lists_hbm, returned_hbm,
+    w_gate, w_up, w_down, units, arrived, dense, lists, picks, part, twin_out, twin_in, far_in, near_in, back,
+    acc, packed, turned, flag_out, flag_in,
+    w_sem, unit_send, unit_recv, own_send, own_recv, fwd_send, fwd_recv, twin_send, twin_recv,
+    part_send, part_recv, far_send, far_recv, near_send, near_recv, part_free, far_free, near_free,
+    back_send, back_recv, flag_send, flag_recv, pull_sem, out_sem,
+):
+    tokens, width = moe_input.shape
+    hid = w_gate.shape[1]
+    half = width // 2
+    full = half + LANES
+    ep = lax.axis_index("ep")
+    fs = lax.axis_index("fsdp")
+    z = lax.rem(fs, 2) * 2 + ep // 8
+    y = lax.rem(ep // 2, 4)
+    core = lax.rem(ep, 2)
+    x = fs // 2
+    mine = z * 2 + core
+    other = 1 - core
+
+    def at(ax, ay, az, ac):
+        return (lax.rem(az, 2) * 8 + ay * 2 + ac, ax * 2 + az // 2)
+
+    def shift(v, n):
+        return lax.rem(v + n, 4)
+
+    plus = at(shift(x, 1), y, z, core)
+    minus = at(shift(x, 3), y, z, core)
+    twin = at(x, y, z, other)
+    remote = functools.partial(pltpu.make_async_remote_copy, device_id_type=MESH)
+    offsets = [(dy, dz, dc) for dy in range(4) for dz in range(4) for dc in range(2)]
+
+    def plane(dy, dz, dc):
+        return shift(y, dy), shift(z, dz), lax.rem(core + dc, 2)
+
+    weights = [
+        pltpu.make_async_copy(w_gate_hbm.at[0], w_gate, w_sem.at[0]),
+        pltpu.make_async_copy(w_up_hbm.at[0], w_up, w_sem.at[1]),
+        pltpu.make_async_copy(w_down_hbm.at[0], w_down, w_sem.at[2]),
+    ]
+    barrier = pltpu.get_barrier_semaphore()
+    partners = [plus, minus] + [at(x, *plane(*o)) for o in offsets[1:]]
+    for partner in partners:
+        pl.semaphore_signal(barrier, 1, device_id=partner, device_id_type=MESH)
+
+    col_id, row_id = ids_col[...], ids_row[...]
+    same = col_id == row_id
+    above = iota((tokens, tokens), 0) < iota((tokens, tokens), 1)
+    below = iota((tokens, tokens), 0) > iota((tokens, tokens), 1)
+    slot_row = jnp.sum((same & above).astype(F32), axis=0, keepdims=True).astype(jnp.int32)
+    slot_col = jnp.sum((same & below).astype(F32), axis=1, keepdims=True).astype(jnp.int32)
+    target = (row_id // 2) * UNIT + (row_id % 2) * CAP + slot_row
+    place = (iota((SLOTS, tokens), 0) == target).astype(F32)
+    taken = jnp.sum(place, axis=1, keepdims=True)
+    place = place.astype(BF)
+    square = (SLOTS, SLOTS)
+    spread = ones(iota(square, 1) == mine * UNIT + iota(square, 0) % UNIT)
+    to_flag = ones(
+        (iota(square, 0) % UNIT == FLAG_ROW) & (iota(square, 0) // UNIT == iota(square, 1) // UNIT)
+    )
+    flags = nn(to_flag, (taken * spread.astype(F32)).astype(BF))
+    gate = gates[...].astype(F32)
+    step = 1024
+
+    def pack(i, carry):
+        cols = pl.ds(pl.multiple_of(i * step, step), step)
+        gated = (gate * out_grad[:, cols].astype(F32)).astype(BF)
+        units[0, :, :, cols] = nn(place, moe_input[:, cols]).astype(BF).reshape(8, UNIT, step)
+        units[1, :, :, cols] = nn(place, gated).astype(BF).reshape(8, UNIT, step)
+        return carry
+
+    lax.fori_loop(0, width // step, pack, 0)
+    for a in range(2):
+        head = units[a, :, :, 0:LANES].reshape(SLOTS, LANES).astype(F32)
+        units[a, :, :, 0:LANES] = (head + flags).astype(BF).reshape(8, UNIT, LANES)
+    from_pair = iota((tokens, 2 * SLOTS), 1)
+    token_map = ones(
+        (from_pair // 64 == (col_id // 2) % 4)
+        & ((from_pair // UNIT) % 2 == col_id // 8)
+        & (from_pair % UNIT == (col_id % 2) * CAP + slot_col)
+    )
+    pl.semaphore_wait(barrier, len(partners))
+
+    unit_copies = []
+
+    def units_out(k):
+        for dz in range(4):
+            for dc in range(2):
+                ay, az, ac = plane((4 - k) % 4, dz, dc)
+                src = units.at[ac, lax.rem(az, 2) * 4 + ay]
+                dst = arrived.at[k * BLOCKS + mine]
+                index = (k * 4 + dz) * 2 + dc
+                sem = unit_recv.at[k * BLOCKS + mine]
+                if k or dz or dc:
+                    copy = remote(src, dst, unit_send.at[index], sem, device_id=at(x, ay, az, ac))
+                    copy.start()
+                    unit_copies.append(copy)
+                else:
+                    pltpu.make_async_copy(src, dst, sem).start()
+
+    earlier = ones(iota(square, 0) < iota(square, 1))
+    owner = iota(square, 0) % UNIT
+    lane = iota(square, 1)
+    whose = ones(((lane == 0) & (owner < CAP)) | ((lane == 1) & (owner >= CAP) & (owner < 2 * CAP)))
+    own, kept, fwd, twins, parts, far, near, backs = ({} for _ in range(8))
+    over = [jnp.zeros((1, 1), F32)]
+
+    def take_in(k):
+        for b in range(BLOCKS):
+            j = k * BLOCKS + b
+            pltpu.make_async_copy(arrived.at[j], arrived.at[j], unit_recv.at[j]).wait()
+        tiles = arrived[k * BLOCKS : (k + 1) * BLOCKS, :, 0:LANES].astype(F32)
+        flag = jnp.where(iota(tiles.shape, 1) == FLAG_ROW, tiles, 0.0)
+        flag = jnp.sum(flag.reshape(SLOTS, LANES), axis=0, keepdims=True)
+        rank = nn(flag.astype(BF), earlier)
+        count = jnp.sum(flag, axis=1, keepdims=True)
+        over[0] = jnp.maximum(over[0], (count > LIST).astype(F32))
+        pick = ones((iota((LIST, SLOTS), 0).astype(F32) == rank) & (flag > 0.5))
+        picks[k] = pick
+        masks = nn(pick, whose) + jnp.where(iota((LIST, LANES), 1) == 2, over[0], 0.0)
+        dense[k, :, width : width + LANES] = masks.astype(BF)
+
+        def move(i, carry):
+            cols = pl.ds(pl.multiple_of(i * step, step), step)
+            found = arrived[k * BLOCKS : (k + 1) * BLOCKS, :, cols].reshape(SLOTS, step)
+            dense[k, :, cols] = nn(pick, found).astype(BF)
+            return carry
+
+        lax.fori_loop(0, width // step, move, 0)
+        to = lists_hbm.at[core, k]
+        own[k] = [
+            remote(dense.at[k], to.at[1], own_send.at[k, 0], own_recv.at[k, 0], device_id=plus),
+            remote(dense.at[k], to.at[2], own_send.at[k, 1], own_recv.at[k, 1], device_id=minus),
+        ]
+        twins[k] = [remote(dense.at[k], to.at[0], twin_send.at[k, 0], twin_recv.at[k, 0], device_id=twin)]
+        kept[k] = pltpu.make_async_copy(dense.at[k], to.at[0], own_send.at[k, 2])
+        for copy in own[k] + twins[k] + [kept[k]]:
+            copy.start()
+
+    def forward(k):
+        to = lists_hbm.at[core, k]
+        cut = 48 if k % 2 == 0 else 32
+        low, high = pl.ds(0, cut), pl.ds(cut, LIST - cut)
+        fwd[k] = [
+            remote(to.at[1, low], to.at[3, low], fwd_send.at[k, 0], fwd_recv.at[k, 0], device_id=plus),
+            remote(to.at[2, high], to.at[3, high], fwd_send.at[k, 1], fwd_recv.at[k, 1], device_id=minus),
+        ]
+        for i in range(2):
+            own[k][i].wait_recv()
+            fwd[k][i].start()
+            copy = remote(to.at[i + 1], to.at[i + 1], twin_send.at[k, i + 1], twin_recv.at[k, i + 1], device_id=twin)
+            copy.start()
+            twins[k].append(copy)
+
+    def share(k):
+        to = lists_hbm.at[core, k]
+        for copy in fwd[k]:
+            copy.wait_recv()
+        copy = remote(to.at[3], to.at[3], twin_send.at[k, 3], twin_recv.at[k, 3], device_id=twin)
+        copy.start()
+        twins[k].append(copy)
+
+    def compute(k):
+        kept[k].wait()
+        for copy in twins[k]:
+            copy.wait_recv()
+        pull = pltpu.make_async_copy(lists_hbm.at[:, k], lists, pull_sem.at[0])
+        pull.start()
+        acc[...] = jnp.zeros_like(acc)
+        pull.wait()
+
+        def gather(i, carry):
+            cols = pl.ds(pl.multiple_of(i * step, step), step)
+            left = lists[0, :, :, cols].reshape(ROWS, step)
+            acc[0:ROWS, 0:hid] += nn(left, w_gate[cols, :])
+            acc[0:ROWS, hid : 2 * hid] += nn(left, w_up[cols, :])
+            acc[0:ROWS, 2 * hid : 3 * hid] += nt(lists[1, :, :, cols].reshape(ROWS, step), w_down[:, cols])
+            return carry
+
+        lax.fori_loop(0, width // step, gather, 0)
+        if k:
+            for copy in [parts[k - 1]] + far[k - 1] + near[k - 1]:
+                copy.wait_send()
+        for r in range(4):
+            rows = slice(r * LIST, (r + 1) * LIST)
+            tile = lists[0, r, :, width : width + LANES].astype(F32)
+            mask = jnp.sum(jnp.where(iota(tile.shape, 1) == core, tile, 0.0), axis=1, keepdims=True)
+            pre_gate = acc[rows, 0:hid]
+            pre_up = acc[rows, hid : 2 * hid]
+            scaled = acc[rows, 2 * hid : 3 * hid] * mask
+            sig = jax.nn.sigmoid(pre_gate)
+            act = pre_gate * sig
+            slope = sig * (1.0 + pre_gate * (1.0 - sig))
+            hidden = (act * pre_up).astype(BF).astype(F32) * mask
+            piece = jnp.sum(hidden * scaled, axis=1, keepdims=True) * (1.0 / math.sqrt(width))
+            acc[rows, 0:hid] = scaled * pre_up * slope
+            acc[rows, hid : 2 * hid] = scaled * act
+            acc[rows, 2 * hid : 3 * hid] = hidden
+            wide = jnp.broadcast_to(piece, (LIST, LANES)).astype(BF)
+            part[r, :, half:full] = wide
+            twin_out[r, :, half:full] = wide
+        turned[k] = jnp.transpose(acc[...]).astype(BF)
+        packed[...] = acc[0:ROWS, 0 : 2 * hid].astype(BF)
+        span = 512
+
+        def rows_back(into, first):
+            def one(i, carry):
+                cols = pl.ds(pl.multiple_of(i * span, span), span)
+                here = pl.ds(pl.multiple_of(first + i * span, span), span)
+                total = nt(packed[:, 0:hid], w_gate[here, :]) + nt(packed[:, hid : 2 * hid], w_up[here, :])
+                into[:, :, cols] = total.astype(BF).reshape(4, LIST, span)
+                return carry
+
+            lax.fori_loop(0, half // span, one, 0)
+
+        rows_back(twin_out, other * half)
+        if k:
+            pl.semaphore_wait(part_free, 1)
+        parts[k] = remote(twin_out, twin_in, part_send.at[k], part_recv.at[k], device_id=twin)
+        parts[k].start()
+        rows_back(part, core * half)
+
+    def merge(k):
+        parts[k].wait_recv()
+
+        def add(r, carry):
+            part[r] = (part[r].astype(F32) + twin_in[r].astype(F32)).astype(BF)
+            return carry
+
+        cut = 48 if k % 2 == 0 else 32
+        low, high = pl.ds(0, cut), pl.ds(cut, LIST - cut)
+        part[3] = (part[3].astype(F32) + twin_in[3].astype(F32)).astype(BF)
+        if k:
+            pl.semaphore_wait(far_free, 2)
+        far[k] = [
+            remote(part.at[3, low], far_in.at[0, low], far_send.at[k, 0], far_recv.at[k, 0], device_id=plus),
+            remote(part.at[3, high], far_in.at[1, high], far_send.at[k, 1], far_recv.at[k, 1], device_id=minus),
+        ]
+        for copy in far[k]:
+            copy.start()
+        lax.fori_loop(0, 3, add, 0)
+        if k < STEPS - 1:
+            pl.semaphore_signal(part_free, 1, device_id=twin, device_id_type=MESH)
+
+    def pass_on(k):
+        if k:
+            pl.semaphore_wait(near_free, 2)
+        near[k] = [
+            remote(part.at[2], near_in.at[0], near_send.at[k, 0], near_recv.at[k, 0], device_id=plus),
+            remote(part.at[1], near_in.at[1], near_send.at[k, 1], near_recv.at[k, 1], device_id=minus),
+        ]
+        cut = 48 if k % 2 == 0 else 32
+        for i, rel, rows, giver in ((0, 2, slice(0, cut), minus), (1, 1, slice(cut, LIST), plus)):
+            far[k][i].wait_recv()
+            part[rel, rows] = (part[rel, rows].astype(F32) + far_in[i, rows].astype(F32)).astype(BF)
+            if k < STEPS - 1:
+                pl.semaphore_signal(far_free, 1, device_id=giver, device_id_type=MESH)
+            near[k][i].start()
+
+    def send_back(k):
+        for copy in near[k]:
+            copy.wait_recv()
+        slot = k % 2
+        if k >= 2:
+            for copy in backs[k - 2]:
+                copy.wait_send()
+        for first in range(0, full, 1024):
+            cols = slice(first, min(first + 1024, full))
+            total = tn(picks[k], part[0, :, cols]) + tn(picks[k], near_in[0, :, cols])
+            total = total + tn(picks[k], near_in[1, :, cols])
+            back[slot, :, :, cols] = total.astype(BF).reshape(BLOCKS, UNIT, cols.stop - cols.start)
+        if k < STEPS - 1:
+            for giver in (minus, plus):
+                pl.semaphore_signal(near_free, 1, device_id=giver, device_id_type=MESH)
+        me = core * 16 + y * 4 + z
+        backs[k] = []
+        for dz in range(4):
+            for dc in range(2):
+                ay, az, ac = plane(k, dz, dc)
+                src = back.at[slot, az * 2 + ac]
+                index = (k * 4 + dz) * 2 + dc
+                if k or dz or dc:
+                    copy = remote(src, returned_hbm.at[me], back_send.at[index], back_recv.at[me], device_id=at(x, ay, az, ac))
+                    copy.start()
+                    backs[k].append(copy)
+                else:
+                    stay = pltpu.make_async_copy(src, returned_hbm.at[me], pull_sem.at[1])
+                    stay.start()
+                    stay.wait()
+
+    flag_copies = []
+
+    def tell():
+        tile = jnp.maximum(lists[0, 0, 0:16, width : width + LANES], lists[0, 1, 0:16, width : width + LANES])
+        tile = jnp.maximum(tile, lists[0, 2, 0:16, width : width + LANES])
+        tile = jnp.maximum(tile, lists[0, 3, 0:16, width : width + LANES]).astype(F32)
+        flag_out[...] = jnp.where(iota(tile.shape, 1) == 2, tile, 0.0).astype(BF)
+        me = y * BLOCKS + mine
+        for i, o in enumerate(offsets):
+            if i:
+                copy = remote(flag_out, flag_in.at[me], flag_send.at[i], flag_recv.at[me], device_id=at(x, *plane(*o)))
+                copy.start()
+                flag_copies.append(copy)
+        flag_in[me] = flag_out[...]
+
+    scale = 1.0 / math.sqrt(tokens * 8)
+    span = 512
+    blocks = width // span
+    out_copies = []
+
+    def stream(i, slot):
+        cols = pl.ds(pl.multiple_of(i * span, span), span)
+        made = []
+        for k in range(STEPS):
+            there = pl.ds(pl.multiple_of((slot * STEPS + k) * span, span), span)
+            made.append(
+                pltpu.make_async_copy(
+                    lists_hbm.at[:, k, :, :, cols], lists.at[:, :, :, there], out_sem.at[slot * STEPS + k]
+                )
+            )
+        return made
+
+    def gradients(first, last):
+        def one(i, carry):
+            slot = lax.rem(i, 2)
+            cols = pl.ds(pl.multiple_of(i * span, span), span)
+
+            @pl.when(i + 1 < blocks)
+            def _():
+                for copy in stream(i + 1, 1 - slot):
+                    copy.start()
+
+            for copy in stream(i, slot):
+                copy.wait()
+            total = jnp.zeros((2 * hid, span), F32)
+            down = jnp.zeros((hid, span), F32)
+            for k in range(STEPS):
+                there = pl.ds(pl.multiple_of((slot * STEPS + k) * span, span), span)
+                total = total + nn(turned[k, 0 : 2 * hid, 0:ROWS], lists[0, :, :, there].reshape(ROWS, span))
+                down = down + nn(turned[k, 2 * hid : 3 * hid, 0:ROWS], lists[1, :, :, there].reshape(ROWS, span))
+            total = total * scale
+            w_gate[cols, :] = jnp.transpose(total[0:hid]).astype(BF)
+            w_up[cols, :] = jnp.transpose(total[hid : 2 * hid]).astype(BF)
+            w_down[:, cols] = (down * scale).astype(BF)
+            return carry
+
+        if first == 0:
+            for copy in stream(0, 0):
+                copy.start()
+        lax.fori_loop(first, last, one, 0)
+        rows = pl.ds(first * span, (last - first) * span)
+        n = 8 + len(out_copies)
+        made = [
+            pltpu.make_async_copy(w_gate.at[rows], grad_gate_hbm.at[0, rows], out_sem.at[n]),
+            pltpu.make_async_copy(w_up.at[rows], grad_up_hbm.at[0, rows], out_sem.at[n + 1]),
+            pltpu.make_async_copy(w_down.at[:, rows], grad_down_hbm.at[0, :, rows], out_sem.at[n + 2]),
+        ]
+        for copy in made:
+            copy.start()
+        out_copies.extend(made)
+
+    units_out(0)
+    for copy in weights:
+        copy.start()
+    take_in(0)
+    units_out(1)
+    take_in(1)
+    units_out(2)
+    units_out(3)
+    forward(0)
+    take_in(2)
+    share(0)
+    forward(1)
+    take_in(3)
+    for copy in weights:
+        copy.wait()
+    compute(0)
+    merge(0)
+    share(1)
+    forward(2)
+    pass_on(0)
+    send_back(0)
+    compute(1)
+    merge(1)
+    share(2)
+    forward(3)
+    pass_on(1)
+    send_back(1)
+    compute(2)
+    merge(2)
+    share(3)
+    pass_on(2)
+    send_back(2)
+    compute(3)
+    tell()
+    merge(3)
+    gradients(0, 3)
+    pass_on(3)
+    gradients(3, 8)
+    send_back(3)
+    gradients(8, 14)
+
+    for dy, dz, dc in offsets[1:]:
+        ay, az, ac = plane(dy, dz, dc)
+        j = ac * 16 + ay * 4 + az
+        pltpu.make_async_copy(back.at[0, 0], returned_hbm.at[j], back_recv.at[j]).wait()
+        j = ay * BLOCKS + az * 2 + ac
+        pltpu.make_async_copy(flag_out, flag_in.at[j], flag_recv.at[j]).wait()
+    pull = pltpu.make_async_copy(returned_hbm, arrived.at[:, :, pl.ds(0, full)], pull_sem.at[0])
+    pull.start()
+    seen = jnp.max(flag_in[...].astype(F32).reshape(32 * 16, LANES), axis=0, keepdims=True)
+    overflow[...] = jnp.broadcast_to(jnp.max(seen, axis=1, keepdims=True), overflow.shape)
+    pull.wait()
+    for h in range(2):
+        for first in range(0, half, 512):
+            found = arrived[h * 16 : (h + 1) * 16, :, first : first + 512].reshape(2 * SLOTS, 512)
+            moe_grad[:, h * half + first : h * half + first + 512] = nn(token_map, found).astype(BF)
+    found = arrived[0:16, :, half:full].reshape(2 * SLOTS, LANES)
+    gate_grad[...] = (nn(token_map, found) / gate).astype(BF)
+
+    for copy in out_copies:
+        copy.wait()
+    for copy in unit_copies + flag_copies + [parts[STEPS - 1]]:
+        copy.wait_send()
+    for k in range(STEPS):
+        for copy in own[k] + fwd[k] + twins[k]:
+            copy.wait_send()
+    for copy in far[STEPS - 1] + near[STEPS - 1] + backs[STEPS - 2] + backs[STEPS - 1]:
+        copy.wait_send()
+
+
+def fast(moe_input, out_grad, expert_ids, gate_values, w_gate, w_up, w_down):
+    tokens, width = moe_input.shape
+    hid = w_gate.shape[2]
+    full = width // 2 + LANES
+    vmem = pl.BlockSpec(memory_space=pltpu.VMEM)
+    anywhere = pl.BlockSpec(memory_space=pl.ANY)
+    dma = pltpu.SemaphoreType.DMA
+    regular = pltpu.SemaphoreType.REGULAR
+    return pl.pallas_call(
+        kernel,
+        out_shape=[
+            jax.ShapeDtypeStruct((tokens, width), BF),
+            jax.ShapeDtypeStruct((tokens, LANES), BF),
+            jax.ShapeDtypeStruct((8, LANES), F32),
+            jax.ShapeDtypeStruct(w_gate.shape, BF),
+            jax.ShapeDtypeStruct(w_up.shape, BF),
+            jax.ShapeDtypeStruct(w_down.shape, BF),
+            jax.ShapeDtypeStruct((2, STEPS, 4, LIST, width + LANES), BF),
+            jax.ShapeDtypeStruct((32, UNIT, full), BF),
+        ],
+        in_specs=[vmem] * 5 + [anywhere] * 3,
+        out_specs=[vmem] * 3 + [anywhere] * 5,
+        scratch_shapes=[
+            pltpu.VMEM((width, hid), BF),
+            pltpu.VMEM((width, hid), BF),
+            pltpu.VMEM((hid, width), BF),
+            pltpu.VMEM((2, 8, UNIT, width), BF),
+            pltpu.VMEM((STEPS * BLOCKS, UNIT, width), BF),
+            pltpu.VMEM((STEPS, LIST, width + LANES), BF),
+            pltpu.VMEM((2, 4, LIST, width + LANES), BF),
+            pltpu.VMEM((STEPS, LIST, SLOTS), BF),
+            pltpu.VMEM((4, LIST, full), BF),
+            pltpu.VMEM((4, LIST, full), BF),
+            pltpu.VMEM((4, LIST, full), BF),
+            pltpu.VMEM((2, LIST, full), BF),
+            pltpu.VMEM((2, LIST, full), BF),
+            pltpu.VMEM((2, BLOCKS, UNIT, full), BF),
+            pltpu.VMEM((PADDED, 3 * hid), F32),
+            pltpu.VMEM((ROWS, 2 * hid), BF),
+            pltpu.VMEM((STEPS, 3 * hid, PADDED), BF),
+            pltpu.VMEM((16, LANES), BF),
+            pltpu.VMEM((32, 16, LANES), BF),
+            dma((3,)),
+            dma((32,)),
+            dma((32,)),
+            dma((STEPS, 3)),
+            dma((STEPS, 2)),
+            dma((STEPS, 2)),
+            dma((STEPS, 2)),
+            dma((STEPS, 4)),
+            dma((STEPS, 4)),
+            dma((STEPS,)),
+            dma((STEPS,)),
+            dma((STEPS, 2)),
+            dma((STEPS, 2)),
+            dma((STEPS, 2)),
+            dma((STEPS, 2)),
+            regular,
+            regular,
+            regular,
+            dma((32,)),
+            dma((32,)),
+            dma((32,)),
+            dma((32,)),
+            dma((2,)),
+            dma((17,)),
+        ],
+        compiler_params=pltpu.CompilerParams(
+            collective_id=0, has_side_effects=True, vmem_limit_bytes=63 * 2**20
+        ),
+    )(moe_input, out_grad, expert_ids, expert_ids.reshape(1, tokens), gate_values, w_gate, w_up, w_down)
 
 
 def silu_parts(value):
@@ -23,7 +566,7 @@
     )
 
 
-def body(moe_input, out_grad, expert_ids, gate_values, w_gate, w_up, w_down):
+def general(moe_input, out_grad, expert_ids, gate_values, w_gate, w_up, w_down):
     tok_rows = moe_input.shape[0]
     width = moe_input.shape[1]
     topw = expert_ids.shape[1]
@@ -123,26 +666,19 @@
     return (moe_grad, gate_grad, grad_w_gate, grad_w_up, grad_w_down)
 
 
+def body(*args):
+    moe_grad, gate_wide, overflow, grad_gate, grad_up, grad_down, _, _ = fast(*args)
+    made = (moe_grad, gate_wide[:, 0:1], grad_gate, grad_up, grad_down)
+    return lax.cond(overflow[0, 0] > 0.0, lambda: general(*args), lambda: made)
+
+
 def solution(mesh):
-    placed = (
-        P(("ep", "fsdp"), None),
-        P(("ep", "fsdp"), None),
-        P(("ep", "fsdp"), None),
-        P(("ep", "fsdp"), None),
-        P("ep", None, "fsdp"),
-        P("ep", None, "fsdp"),
-        P("ep", "fsdp", None),
-    )
+    rows = P(("ep", "fsdp"), None)
+    columns = P("ep", None, "fsdp")
     return jax.shard_map(
         body,
         mesh=mesh,
-        in_specs=placed,
-        out_specs=(
-            P(("ep", "fsdp"), None),
-            P(("ep", "fsdp"), None),
-            P("ep", None, "fsdp"),
-            P("ep", None, "fsdp"),
-            P("ep", "fsdp", None),
-        ),
+        in_specs=(rows, rows, rows, rows, columns, columns, P("ep", "fsdp", None)),
+        out_specs=(rows, rows, columns, columns, P("ep", "fsdp", None)),
         check_vma=False,
     )

time: 731 us -> 421 us (0.58)
  waiting for transfers between devices: 403 us -> 0 us
  Pallas kernels: 0 us -> 389 us
  blocking collectives: 112 us -> 0 us
  matrix products: 92 us -> 0 us
  local copies, waits for them, and re-layouts: 80.4 us -> 14.3 us
  starting transfers between devices: 17.3 us -> 0 us
    pallas_call x0 -> x1, Pallas kernels: none -> 389 us  [fast(): pl.pallas_call(kernel, out_shape=[jax.ShapeDtypeStruct((tokens, width), B...]
    all_gather x2 -> x0, waiting for transfers between devices: 245 us -> none  [the longest x1 128 us: body(): piece_grad = lax.all_gather(recv_grad, 'fsdp', axis=0, tiled=True)]
    reduce_scatter x1 -> x0, waiting for transfers between devices: 147 us -> none  [body(): lax.psum_scatter(part_rows.astype(jnp.bfloat16), 'fsdp', scatter_dimensio...]
    dot_general x11 -> x0, matrix products: 92 us -> none  [the longest x3 42.1 us: contract_cols(): lax.dot_general(left, right, (((1,), (1,)), ((), ())), preferred_element_...]
    all_to_all x3 -> x0, blocking collectives: 67.8 us -> none  [the longest x1 30.8 us: body(): lax.all_to_all(send_input, 'ep', split_axis=0, concat_axis=0, tiled=True)]
    reshape x6 -> x0, local copies, waits for them, and re-layouts: 42.5 us -> none  [the longest x1 17.4 us: body(): rows_grad = piece_grad.reshape(count, width)]
    all_gather x2 -> x0, local copies, waits for them, and re-layouts: 31.8 us -> none  [the longest x1 16 us: body(): piece_grad = lax.all_gather(recv_grad, 'fsdp', axis=0, tiled=True)]
    all_gather x1 -> x0, blocking collectives: 27.8 us -> none  [body(): piece_gate = lax.all_gather(recv_gate, 'fsdp', axis=0, tiled=True)]
  transfers between devices with their start and end apart: 5 -> 0, of which waited for: 5 -> 0; matrix products, arithmetic and copies ran while one was open for 9% -> 0% of each run, Pallas kernels for 0% -> 0%
where the time goes in v2:
time: 421 us; the launch traced here: 419 us
  Pallas kernels  389 us (92%)
  between operations  14.7 us (3%)
  local copies, waits for them, and re-layouts  14.3 us (3%)
    pallas_call x1, Pallas kernels, fast(): pl.pallas_call(kernel, out_shape=[jax.ShapeDtypeStruct((tokens, width), B...  389 us
    unnamed x16, local copies, waits for them, and re-layouts  13 us

profile of v2, /device:TPU:41, one launch (start us, length us, event | category | flops | bytes accessed | tf_op | source)
XLA Modules:
  0.0 418.7 jit_solution(2074880514277987977)
XLA Ops:
  7.2 1.4 copy.45.gates
  8.5 1.3 copy.44.ids_col
  9.9 0.0 copy-start.5
  9.9 0.0 copy-start.6
  9.9 389.4 %shard_map.112 = (bf16[36,7168]{1,0:T(8,128)(2,1)S(1)}, bf16[36,128]{1,0:T(8,128)(2,1)S(1)}, f32[8,128]{1,0:T(8,128)}, bf16[1,7168,256]{2,1,0:T(8,128)(2,1)}, bf...) custom-call(bf16[36,7168]{1,0:T(8,128)(2,1)} %moe_input.1, ...), custom_call_target="tpu_custom_call" | custom-call | tf_op jit(solution)/shard_map/pallas_call | solution.py:487
  399.3 1.2 slice.7
  401.1 0.0 copy-done.5
  401.2 0.0 copy-done.6
  401.2 0.4 conditional.1
  401.2 0.1 copy.46
  401.6 0.0 copy-start.8
  401.6 0.8 copy.61
  402.4 0.0 copy-start.3
  402.4 4.3 %copy.62 = bf16[1,7168,256]{2,1,0:T(8,128)(2,1)} copy(bf16[1,7168,256]{2,1,0:T(8,128)(2,1)} %get-tuple-element.109) | data formatting | bytes 7340032
  406.7 0.0 copy-done.8
  406.7 0.0 copy-done.3
  406.7 0.0 copy-start.2
  406.7 1.9 copy.63
  408.5 1.5 copy-done.2
  410.0 1.8 copy.64
  (1 shorter events, 0.0 us)
Async XLA Ops:
  9.9 391.3 %copy-start.5 = (s32[36,1]{0,1:T(1,128)S(1)}, s32[36,1]{0,1:T(1,128)}, u32[]{:S(2)}) copy-start(s32[36,1]{0,1:T(1,128)} %param.11) | copy-start | bytes 436
  9.9 391.3 %copy-start.6 = (bf16[36,1]{0,1:T(2,128)(2,1)S(1)}, bf16[36,1]{0,1:T(2,128)(2,1)}, u32[]{:S(2)}) copy-start(bf16[36,1]{0,1:T(2,128)(2,1)} %param.12) | copy-start | bytes 220
  401.6 5.1 %copy-start.8 = (bf16[36,1]{0,1:T(2,128)(2,1)}, bf16[36,1]{0,1:T(2,128)(2,1)S(1)}, u32[]{:S(2)}) copy-start(bf16[36,1]{0,1:T(2,128)(2,1)S(1)} %get-tuple-element.108) | copy-start | bytes 220
  402.4 4.3 %copy-start.3 = (bf16[1,7168,256]{2,1,0:T(8,128)(2,1)S(1)}, bf16[1,7168,256]{2,1,0:T(8,128)(2,1)}, u32[]{:S(2)}) copy-start(bf16[1,7168,256]{2,1,0:T(8,128)(2,1)} %get-tuple-element.110) | copy-start | bytes 11010052
  406.7 3.4 copy-start.2

commit v3 on v2

--- a/solution.py
+++ b/solution.py
@@ -44,11 +44,11 @@
 
 
 def kernel(
-    moe_input, out_grad, ids_col, ids_row, gates, w_gate_hbm, w_up_hbm, w_down_hbm,
+    moe_input, out_grad, ids, gates, w_gate_hbm, w_up_hbm, w_down_hbm,
     moe_grad, gate_grad, overflow, grad_gate_hbm, grad_up_hbm, grad_down_hbm, lists_hbm, returned_hbm,
-    w_gate, w_up, w_down, units, arrived, dense, lists, picks, part, twin_out, twin_in, far_in, near_in, back,
+    w_gate, w_up, w_down, units, relay, arrived, dense, lists, picks, all_part, twin_out, twin_in, far_in, near_in, back,
     acc, packed, turned, flag_out, flag_in,
-    w_sem, unit_send, unit_recv, own_send, own_recv, fwd_send, fwd_recv, twin_send, twin_recv,
+    w_sem, y_send, y_recv, unit_send, unit_recv, own_send, own_recv, fwd_send, fwd_recv, twin_send, twin_recv,
     part_send, part_recv, far_send, far_recv, near_send, near_recv, part_free, far_free, near_free,
     back_send, back_recv, flag_send, flag_recv, pull_sem, out_sem,
 ):
@@ -85,18 +85,27 @@
         pltpu.make_async_copy(w_up_hbm.at[0], w_up, w_sem.at[1]),
         pltpu.make_async_copy(w_down_hbm.at[0], w_down, w_sem.at[2]),
     ]
+    for copy in weights:
+        copy.start()
     barrier = pltpu.get_barrier_semaphore()
     partners = [plus, minus] + [at(x, *plane(*o)) for o in offsets[1:]]
     for partner in partners:
         pl.semaphore_signal(barrier, 1, device_id=partner, device_id_type=MESH)
 
-    col_id, row_id = ids_col[...], ids_row[...]
+    token_square = (tokens, tokens)
+    diagonal = iota(token_square, 0) == iota(token_square, 1)
+
+    def upright(row):
+        return jnp.sum(jnp.where(diagonal, row, 0.0), axis=1, keepdims=True)
+
+    row_id = ids[...]
+    col_id = upright(row_id.astype(F32)).astype(jnp.int32)
     same = col_id == row_id
     above = iota((tokens, tokens), 0) < iota((tokens, tokens), 1)
     below = iota((tokens, tokens), 0) > iota((tokens, tokens), 1)
     slot_row = jnp.sum((same & above).astype(F32), axis=0, keepdims=True).astype(jnp.int32)
     slot_col = jnp.sum((same & below).astype(F32), axis=1, keepdims=True).astype(jnp.int32)
-    target = (row_id // 2) * UNIT + (row_id % 2) * CAP + slot_row
+    target = ((row_id // 2) % 4 * 2 + row_id // 8) * UNIT + (row_id % 2) * CAP + slot_row
     place = (iota((SLOTS, tokens), 0) == target).astype(F32)
     taken = jnp.sum(place, axis=1, keepdims=True)
     place = place.astype(BF)
@@ -106,20 +115,20 @@
         (iota(square, 0) % UNIT == FLAG_ROW) & (iota(square, 0) // UNIT == iota(square, 1) // UNIT)
     )
     flags = nn(to_flag, (taken * spread.astype(F32)).astype(BF))
-    gate = gates[...].astype(F32)
+    gate = upright(gates[...].astype(F32))
     step = 1024
 
     def pack(i, carry):
         cols = pl.ds(pl.multiple_of(i * step, step), step)
         gated = (gate * out_grad[:, cols].astype(F32)).astype(BF)
-        units[0, :, :, cols] = nn(place, moe_input[:, cols]).astype(BF).reshape(8, UNIT, step)
-        units[1, :, :, cols] = nn(place, gated).astype(BF).reshape(8, UNIT, step)
+        units[:, 0, :, :, cols] = nn(place, moe_input[:, cols]).astype(BF).reshape(4, 2, UNIT, step)
+        units[:, 1, :, :, cols] = nn(place, gated).astype(BF).reshape(4, 2, UNIT, step)
         return carry
 
     lax.fori_loop(0, width // step, pack, 0)
     for a in range(2):
-        head = units[a, :, :, 0:LANES].reshape(SLOTS, LANES).astype(F32)
-        units[a, :, :, 0:LANES] = (head + flags).astype(BF).reshape(8, UNIT, LANES)
+        head = units[:, a, :, :, 0:LANES].reshape(SLOTS, LANES).astype(F32)
+        units[:, a, :, :, 0:LANES] = (head + flags).astype(BF).reshape(4, 2, UNIT, LANES)
     from_pair = iota((tokens, 2 * SLOTS), 1)
     token_map = ones(
         (from_pair // 64 == (col_id // 2) % 4)
@@ -130,16 +139,27 @@
 
     unit_copies = []
 
+    over_y = {}
+
+    def units_over(k):
+        ay = shift(y, 4 - k)
+        over_y[k] = remote(units.at[ay], relay.at[k - 1], y_send.at[k], y_recv.at[k], device_id=at(x, ay, z, core))
+        over_y[k].start()
+        unit_copies.append(over_y[k])
+
     def units_out(k):
+        if k:
+            over_y[k].wait_recv()
         for dz in range(4):
             for dc in range(2):
-                ay, az, ac = plane((4 - k) % 4, dz, dc)
-                src = units.at[ac, lax.rem(az, 2) * 4 + ay]
+                _, az, ac = plane(0, dz, dc)
+                low = lax.rem(az, 2)
+                src = relay.at[k - 1, ac, low] if k else units.at[y, ac, low]
                 dst = arrived.at[k * BLOCKS + mine]
                 index = (k * 4 + dz) * 2 + dc
                 sem = unit_recv.at[k * BLOCKS + mine]
-                if k or dz or dc:
-                    copy = remote(src, dst, unit_send.at[index], sem, device_id=at(x, ay, az, ac))
+                if dz or dc:
+                    copy = remote(src, dst, unit_send.at[index], sem, device_id=at(x, y, az, ac))
                     copy.start()
                     unit_copies.append(copy)
                 else:
@@ -225,8 +245,11 @@
             return carry
 
         lax.fori_loop(0, width // step, gather, 0)
+        part = all_part.at[k % 3]
         if k:
-            for copy in [parts[k - 1]] + far[k - 1] + near[k - 1]:
+            parts[k - 1].wait_send()
+        if k >= 3:
+            for copy in far[k - 3] + near[k - 3]:
                 copy.wait_send()
         for r in range(4):
             rows = slice(r * LIST, (r + 1) * LIST)
@@ -268,6 +291,7 @@
         rows_back(part, core * half)
 
     def merge(k):
+        part = all_part.at[k % 3]
         parts[k].wait_recv()
 
         def add(r, carry):
@@ -290,6 +314,7 @@
             pl.semaphore_signal(part_free, 1, device_id=twin, device_id_type=MESH)
 
     def pass_on(k):
+        part = all_part.at[k % 3]
         if k:
             pl.semaphore_wait(near_free, 2)
         near[k] = [
@@ -305,6 +330,7 @@
             near[k][i].start()
 
     def send_back(k):
+        part = all_part.at[k % 3]
         for copy in near[k]:
             copy.wait_recv()
         slot = k % 2
@@ -407,17 +433,17 @@
         out_copies.extend(made)
 
     units_out(0)
-    for copy in weights:
-        copy.start()
+    for k in range(1, STEPS):
+        units_over(k)
     take_in(0)
     units_out(1)
     take_in(1)
     units_out(2)
-    units_out(3)
     forward(0)
     take_in(2)
+    units_out(3)
+    forward(1)
     share(0)
-    forward(1)
     take_in(3)
     for copy in weights:
         copy.wait()
@@ -425,23 +451,23 @@
     merge(0)
     share(1)
     forward(2)
+    compute(1)
     pass_on(0)
-    send_back(0)
-    compute(1)
     merge(1)
     share(2)
     forward(3)
+    compute(2)
+    send_back(0)
     pass_on(1)
-    send_back(1)
-    compute(2)
     merge(2)
     share(3)
-    pass_on(2)
-    send_back(2)
     compute(3)
     tell()
+    send_back(1)
+    pass_on(2)
     merge(3)
     gradients(0, 3)
+    send_back(2)
     pass_on(3)
     gradients(3, 8)
     send_back(3)
@@ -463,7 +489,8 @@
             found = arrived[h * 16 : (h + 1) * 16, :, first : first + 512].reshape(2 * SLOTS, 512)
             moe_grad[:, h * half + first : h * half + first + 512] = nn(token_map, found).astype(BF)
     found = arrived[0:16, :, half:full].reshape(2 * SLOTS, LANES)
-    gate_grad[...] = (nn(token_map, found) / gate).astype(BF)
+    sums = nn(token_map, found)[:, 0:1] / gate
+    gate_grad[...] = jnp.sum(jnp.where(diagonal, sums, 0.0), axis=0, keepdims=True).astype(BF)
 
     for copy in out_copies:
         copy.wait()
@@ -472,7 +499,10 @@
     for k in range(STEPS):
         for copy in own[k] + fwd[k] + twins[k]:
             copy.wait_send()
-    for copy in far[STEPS - 1] + near[STEPS - 1] + backs[STEPS - 2] + backs[STEPS - 1]:
+    for k in range(STEPS - 3, STEPS):
+        for copy in far[k] + near[k]:
+            copy.wait_send()
+    for copy in backs[STEPS - 2] + backs[STEPS - 1]:
         copy.wait_send()
 
 
@@ -488,7 +518,7 @@
         kernel,
         out_shape=[
             jax.ShapeDtypeStruct((tokens, width), BF),
-            jax.ShapeDtypeStruct((tokens, LANES), BF),
+            jax.ShapeDtypeStruct((1, tokens), BF),
             jax.ShapeDtypeStruct((8, LANES), F32),
             jax.ShapeDtypeStruct(w_gate.shape, BF),
             jax.ShapeDtypeStruct(w_up.shape, BF),
@@ -496,18 +526,19 @@
             jax.ShapeDtypeStruct((2, STEPS, 4, LIST, width + LANES), BF),
             jax.ShapeDtypeStruct((32, UNIT, full), BF),
         ],
-        in_specs=[vmem] * 5 + [anywhere] * 3,
+        in_specs=[vmem] * 4 + [anywhere] * 3,
         out_specs=[vmem] * 3 + [anywhere] * 5,
         scratch_shapes=[
             pltpu.VMEM((width, hid), BF),
             pltpu.VMEM((width, hid), BF),
             pltpu.VMEM((hid, width), BF),
-            pltpu.VMEM((2, 8, UNIT, width), BF),
+            pltpu.VMEM((4, 2, 2, UNIT, width), BF),
+            pltpu.VMEM((STEPS - 1, 2, 2, UNIT, width), BF),
             pltpu.VMEM((STEPS * BLOCKS, UNIT, width), BF),
             pltpu.VMEM((STEPS, LIST, width + LANES), BF),
             pltpu.VMEM((2, 4, LIST, width + LANES), BF),
             pltpu.VMEM((STEPS, LIST, SLOTS), BF),
-            pltpu.VMEM((4, LIST, full), BF),
+            pltpu.VMEM((3, 4, LIST, full), BF),
             pltpu.VMEM((4, LIST, full), BF),
             pltpu.VMEM((4, LIST, full), BF),
             pltpu.VMEM((2, LIST, full), BF),
@@ -519,6 +550,8 @@
             pltpu.VMEM((16, LANES), BF),
             pltpu.VMEM((32, 16, LANES), BF),
             dma((3,)),
+            dma((STEPS,)),
+            dma((STEPS,)),
             dma((32,)),
             dma((32,)),
             dma((STEPS, 3)),
@@ -546,7 +579,7 @@
         compiler_params=pltpu.CompilerParams(
             collective_id=0, has_side_effects=True, vmem_limit_bytes=63 * 2**20
         ),
-    )(moe_input, out_grad, expert_ids, expert_ids.reshape(1, tokens), gate_values, w_gate, w_up, w_down)
+    )(moe_input, out_grad, expert_ids.reshape(1, tokens), gate_values.reshape(1, tokens), w_gate, w_up, w_down)
 
 
 def silu_parts(value):
@@ -608,9 +641,20 @@
     weight_down = w_down[0]
     expert_scale = 1.0 / math.sqrt(tok_rows * groups)
     gate_scale = 1.0 / math.sqrt(width)
-    piece_input = lax.all_gather(recv_input, "fsdp", axis=0, tiled=True)
-    piece_grad = lax.all_gather(recv_grad, "fsdp", axis=0, tiled=True)
-    piece_gate = lax.all_gather(recv_gate, "fsdp", axis=0, tiled=True)
+
+    def gathered(own):
+        copies = jnp.broadcast_to(own[None], (groups,) + own.shape)
+        copies = lax.all_to_all(copies, "fsdp", split_axis=0, concat_axis=0, tiled=True)
+        return copies.reshape((groups * own.shape[0],) + own.shape[1:])
+
+    def summed(pieces):
+        spread = lax.all_to_all(pieces, "fsdp", split_axis=0, concat_axis=0, tiled=True)
+        spread = spread.reshape((groups, pieces.shape[0] // groups) + pieces.shape[1:])
+        return jnp.sum(spread.astype(jnp.float32), axis=0)
+
+    piece_input = gathered(recv_input)
+    piece_grad = gathered(recv_grad)
+    piece_gate = gathered(recv_gate)
     count = piece_input.shape[0] * piece_input.shape[1]
     rows_in = piece_input.reshape(count, width)
     rows_grad = piece_grad.reshape(count, width)
@@ -641,14 +685,8 @@
     grad_w_gate = (acc_gate * expert_scale).astype(jnp.bfloat16)[None]
     grad_w_up = (acc_up * expert_scale).astype(jnp.bfloat16)[None]
     grad_w_down = (acc_down * expert_scale).astype(jnp.bfloat16)[None]
-    summed_rows, summed_gate = (
-        lax.psum_scatter(
-            part_rows.astype(jnp.bfloat16), "fsdp", scatter_dimension=0, tiled=True
-        ).astype(jnp.float32),
-        lax.psum_scatter(
-            part_gate.astype(jnp.bfloat16), "fsdp", scatter_dimension=0, tiled=True
-        ).astype(jnp.float32),
-    )
+    summed_rows = summed(part_rows.astype(jnp.bfloat16))
+    summed_gate = summed(part_gate.astype(jnp.bfloat16))
     back_rows = summed_rows.astype(jnp.bfloat16).reshape(experts, capacity, width)
     back_gate = summed_gate.astype(jnp.bfloat16).reshape(experts, capacity)
     ret_rows, ret_gate = (
@@ -667,8 +705,8 @@
 
 
 def body(*args):
-    moe_grad, gate_wide, overflow, grad_gate, grad_up, grad_down, _, _ = fast(*args)
-    made = (moe_grad, gate_wide[:, 0:1], grad_gate, grad_up, grad_down)
+    moe_grad, gate_row, overflow, grad_gate, grad_up, grad_down, _, _ = fast(*args)
+    made = (moe_grad, gate_row.reshape(-1, 1), grad_gate, grad_up, grad_down)
     return lax.cond(overflow[0, 0] > 0.0, lambda: general(*args), lambda: made)
 
 

time: 421 us -> 313 us (0.74)
  Pallas kernels: 389 us -> 297 us
  between operations: 14.7 us -> 1.35 us
    pallas_call x1, Pallas kernels: 389 us -> 297 us  [fast(): pl.pallas_call(kernel, out_shape=[jax.ShapeDtypeStruct((tokens, width), B...]
    unnamed x16 -> x15, local copies, waits for them, and re-layouts: 13 us -> 11.9 us
where the time goes in v3:
time: 313 us; the launch traced here: 312 us
  Pallas kernels  297 us (95%)
  local copies, waits for them, and re-layouts  13.1 us (4%)
    pallas_call x1, Pallas kernels, fast(): pl.pallas_call(kernel, out_shape=[jax.ShapeDtypeStruct((tokens, width), B...  297 us
    unnamed x15, local copies, waits for them, and re-layouts  11.9 us

profile of v3, /device:TPU:41, one launch (start us, length us, event | category | flops | bytes accessed | tf_op | source)
XLA Modules:
  0.0 311.6 jit_solution(12342234042768047699)
XLA Ops:
  0.6 0.0 copy-start.5
  0.6 0.0 copy-start.6
  0.7 0.0 copy-start.7
  0.7 296.9 %shard_map.112 = (bf16[36,7168]{1,0:T(8,128)(2,1)}, bf16[1,36]{1,0:T(2,128)(2,1)S(1)}, f32[8,128]{1,0:T(8,128)}, bf16[1,7168,256]{2,1,0:T(8,128)(2,1)}, bf16[1,7...) custom-call(bf16[36,7168]{1,0:T(8,128)(2,1)} %moe_input.1, ...), custom_call_target="tpu_custom_call" | custom-call | tf_op jit(solution)/shard_map/pallas_call | solution.py:517
  297.6 1.2 slice.3
  299.5 0.0 copy-done.5
  299.5 0.0 copy-done.6
  299.5 0.0 copy-done.7
  299.5 0.3 conditional.1
  299.8 1.9 copy.62
  301.7 0.5 copy.63
  302.2 0.0 copy-start.4
  302.2 4.3 %copy.64 = bf16[1,7168,256]{2,1,0:T(8,128)(2,1)} copy(bf16[1,7168,256]{2,1,0:T(8,128)(2,1)} %get-tuple-element.89) | data formatting | bytes 7340032
  306.4 0.0 copy-done.4
  306.4 0.0 copy-start.3
  306.4 1.9 copy.65
  308.3 1.5 copy-done.3
  309.8 1.8 copy.66
Async XLA Ops:
  0.6 298.8 %copy-start.5 = (bf16[36,7168]{1,0:T(8,128)(2,1)S(1)}, bf16[36,7168]{1,0:T(8,128)(2,1)}, u32[]{:S(2)}) copy-start(bf16[36,7168]{1,0:T(8,128)(2,1)} %out_grad.1) | copy-start | bytes 1548292
  0.6 298.8 %copy-start.6 = (s32[36,1]{0,1:T(1,128)S(1)}, s32[36,1]{0,1:T(1,128)}, u32[]{:S(2)}) copy-start(s32[36,1]{0,1:T(1,128)} %param.11) | copy-start | bytes 436
  0.7 298.8 %copy-start.7 = (bf16[36,1]{0,1:T(2,128)(2,1)S(1)}, bf16[36,1]{0,1:T(2,128)(2,1)}, u32[]{:S(2)}) copy-start(bf16[36,1]{0,1:T(2,128)(2,1)} %param.12) | copy-start | bytes 220
  302.2 4.3 %copy-start.4 = (bf16[1,7168,256]{2,1,0:T(8,128)(2,1)S(1)}, bf16[1,7168,256]{2,1,0:T(8,128)(2,1)}, u32[]{:S(2)}) copy-start(bf16[1,7168,256]{2,1,0:T(8,128)(2,1)} %get-tuple-element.90) | copy-start | bytes 11010052
  306.4 3.4 %copy-start.3 = (bf16[1,256,7168]{2,1,0:T(8,128)(2,1)S(1)}, bf16[1,256,7168]{2,1,0:T(8,128)(2,1)}, u32[]{:S(2)}) copy-start(bf16[1,256,7168]{2,1,0:T(8,128)(2,1)} %get-tuple-element.91) | copy-start | bytes 11010052

commit v4 on v3

--- a/solution.py
+++ b/solution.py
@@ -20,6 +20,7 @@
 ROWS = 4 * LIST
 PADDED = 384
 LANES = 128
+OVER_Z = (0, 1)
 MESH = pl.DeviceIdType.MESH
 
 
@@ -46,10 +47,11 @@
 def kernel(
     moe_input, out_grad, ids, gates, w_gate_hbm, w_up_hbm, w_down_hbm,
     moe_grad, gate_grad, overflow, grad_gate_hbm, grad_up_hbm, grad_down_hbm, lists_hbm, returned_hbm,
-    w_gate, w_up, w_down, units, relay, arrived, dense, lists, picks, all_part, twin_out, twin_in, far_in, near_in, back,
+    w_gate, w_up, w_down, units, relay, arrived, all_dense, lists, picks, all_part, twin_out, twin_in, z_in, all_far, all_near, back,
     acc, packed, turned, flag_out, flag_in,
     w_sem, y_send, y_recv, unit_send, unit_recv, own_send, own_recv, fwd_send, fwd_recv, twin_send, twin_recv,
-    part_send, part_recv, far_send, far_recv, near_send, near_recv, part_free, far_free, near_free,
+    part_send, part_recv, z_send, z_recv, far_send, far_recv, near_send, near_recv,
+    part_free, z_free, far_free, near_free,
     back_send, back_recv, flag_send, flag_recv, pull_sem, out_sem,
 ):
     tokens, width = moe_input.shape
@@ -74,6 +76,11 @@
     plus = at(shift(x, 1), y, z, core)
     minus = at(shift(x, 3), y, z, core)
     twin = at(x, y, z, other)
+    high = z // 2
+    far_z = at(x, y, shift(z, 2), core)
+    keep = (full // LANES + 1) // 2 * LANES
+    kept_cols = pl.ds(pl.multiple_of(high * (full - keep), LANES), keep)
+    sent_cols = pl.ds(pl.multiple_of((1 - high) * (full - keep), LANES), keep)
     remote = functools.partial(pltpu.make_async_remote_copy, device_id_type=MESH)
     offsets = [(dy, dz, dc) for dy in range(4) for dz in range(4) for dc in range(2)]
 
@@ -169,13 +176,18 @@
     owner = iota(square, 0) % UNIT
     lane = iota(square, 1)
     whose = ones(((lane == 0) & (owner < CAP)) | ((lane == 1) & (owner >= CAP) & (owner < 2 * CAP)))
-    own, kept, fwd, twins, parts, far, near, backs = ({} for _ in range(8))
+    own, kept, fwd, twins, parts, zs, far, near, backs = ({} for _ in range(9))
     over = [jnp.zeros((1, 1), F32)]
 
     def take_in(k):
         for b in range(BLOCKS):
             j = k * BLOCKS + b
             pltpu.make_async_copy(arrived.at[j], arrived.at[j], unit_recv.at[j]).wait()
+        dense = all_dense.at[k % 2]
+        if k >= 2:
+            for copy in own[k - 2] + twins[k - 2][:1]:
+                copy.wait_send()
+            kept[k - 2].wait()
         tiles = arrived[k * BLOCKS : (k + 1) * BLOCKS, :, 0:LANES].astype(F32)
         flag = jnp.where(iota(tiles.shape, 1) == FLAG_ROW, tiles, 0.0)
         flag = jnp.sum(flag.reshape(SLOTS, LANES), axis=0, keepdims=True)
@@ -185,22 +197,22 @@
         pick = ones((iota((LIST, SLOTS), 0).astype(F32) == rank) & (flag > 0.5))
         picks[k] = pick
         masks = nn(pick, whose) + jnp.where(iota((LIST, LANES), 1) == 2, over[0], 0.0)
-        dense[k, :, width : width + LANES] = masks.astype(BF)
+        dense[:, width : width + LANES] = masks.astype(BF)
 
         def move(i, carry):
             cols = pl.ds(pl.multiple_of(i * step, step), step)
             found = arrived[k * BLOCKS : (k + 1) * BLOCKS, :, cols].reshape(SLOTS, step)
-            dense[k, :, cols] = nn(pick, found).astype(BF)
+            dense[:, cols] = nn(pick, found).astype(BF)
             return carry
 
         lax.fori_loop(0, width // step, move, 0)
         to = lists_hbm.at[core, k]
         own[k] = [
-            remote(dense.at[k], to.at[1], own_send.at[k, 0], own_recv.at[k, 0], device_id=plus),
-            remote(dense.at[k], to.at[2], own_send.at[k, 1], own_recv.at[k, 1], device_id=minus),
+            remote(dense, to.at[1], own_send.at[k, 0], own_recv.at[k, 0], device_id=plus),
+            remote(dense, to.at[2], own_send.at[k, 1], own_recv.at[k, 1], device_id=minus),
         ]
-        twins[k] = [remote(dense.at[k], to.at[0], twin_send.at[k, 0], twin_recv.at[k, 0], device_id=twin)]
-        kept[k] = pltpu.make_async_copy(dense.at[k], to.at[0], own_send.at[k, 2])
+        twins[k] = [remote(dense, to.at[0], twin_send.at[k, 0], twin_recv.at[k, 0], device_id=twin)]
+        kept[k] = pltpu.make_async_copy(dense, to.at[0], own_send.at[k, 2])
         for copy in own[k] + twins[k] + [kept[k]]:
             copy.start()
 
@@ -228,7 +240,8 @@
         twins[k].append(copy)
 
     def compute(k):
-        kept[k].wait()
+        if k >= 2:
+            kept[k].wait()
         for copy in twins[k]:
             copy.wait_recv()
         pull = pltpu.make_async_copy(lists_hbm.at[:, k], lists, pull_sem.at[0])
@@ -290,6 +303,24 @@
         parts[k].start()
         rows_back(part, core * half)
 
+    def window(k):
+        return (kept_cols, pl.ds(0, keep)) if k in OVER_Z else (pl.ds(0, full), pl.ds(0, full))
+
+    def start_far(k):
+        part = all_part.at[k % 3]
+        far_in = all_far.at[k % 2]
+        here, there = window(k)
+        cut = 48 if k % 2 == 0 else 32
+        low, up = pl.ds(0, cut), pl.ds(cut, LIST - cut)
+        if k >= 2:
+            pl.semaphore_wait(far_free.at[k % 2], 2)
+        far[k] = [
+            remote(part.at[3, low, here], far_in.at[0, low, there], far_send.at[k, 0], far_recv.at[k, 0], device_id=plus),
+            remote(part.at[3, up, here], far_in.at[1, up, there], far_send.at[k, 1], far_recv.at[k, 1], device_id=minus),
+        ]
+        for copy in far[k]:
+            copy.start()
+
     def merge(k):
         part = all_part.at[k % 3]
         parts[k].wait_recv()
@@ -298,53 +329,78 @@
             part[r] = (part[r].astype(F32) + twin_in[r].astype(F32)).astype(BF)
             return carry
 
-        cut = 48 if k % 2 == 0 else 32
-        low, high = pl.ds(0, cut), pl.ds(cut, LIST - cut)
-        part[3] = (part[3].astype(F32) + twin_in[3].astype(F32)).astype(BF)
-        if k:
-            pl.semaphore_wait(far_free, 2)
-        far[k] = [
-            remote(part.at[3, low], far_in.at[0, low], far_send.at[k, 0], far_recv.at[k, 0], device_id=plus),
-            remote(part.at[3, high], far_in.at[1, high], far_send.at[k, 1], far_recv.at[k, 1], device_id=minus),
-        ]
-        for copy in far[k]:
-            copy.start()
-        lax.fori_loop(0, 3, add, 0)
+        if k in OVER_Z:
+            lax.fori_loop(0, 4, add, 0)
+            if k != OVER_Z[0]:
+                pl.semaphore_wait(z_free, 1)
+            zs[k] = remote(part.at[:, :, sent_cols], z_in, z_send.at[k], z_recv.at[k], device_id=far_z)
+            zs[k].start()
+        else:
+            add(3, 0)
+            start_far(k)
+            lax.fori_loop(0, 3, add, 0)
         if k < STEPS - 1:
             pl.semaphore_signal(part_free, 1, device_id=twin, device_id_type=MESH)
 
+    def add_z(k):
+        part = all_part.at[k % 3]
+        zs[k].wait()
+
+        def add(r, carry):
+            part[r, :, kept_cols] = (part[r, :, kept_cols].astype(F32) + z_in[r].astype(F32)).astype(BF)
+            return carry
+
+        lax.fori_loop(0, 4, add, 0)
+        if k != OVER_Z[-1]:
+            pl.semaphore_signal(z_free, 1, device_id=far_z, device_id_type=MESH)
+        start_far(k)
+
     def pass_on(k):
         part = all_part.at[k % 3]
-        if k:
-            pl.semaphore_wait(near_free, 2)
+        far_in, near_in = all_far.at[k % 2], all_near.at[k % 2]
+        here, there = window(k)
+        if k >= 2:
+            pl.semaphore_wait(near_free.at[k % 2], 2)
         near[k] = [
-            remote(part.at[2], near_in.at[0], near_send.at[k, 0], near_recv.at[k, 0], device_id=plus),
-            remote(part.at[1], near_in.at[1], near_send.at[k, 1], near_recv.at[k, 1], device_id=minus),
+            remote(part.at[2, :, here], near_in.at[0, :, there], near_send.at[k, 0], near_recv.at[k, 0], device_id=plus),
+            remote(part.at[1, :, here], near_in.at[1, :, there], near_send.at[k, 1], near_recv.at[k, 1], device_id=minus),
         ]
         cut = 48 if k % 2 == 0 else 32
         for i, rel, rows, giver in ((0, 2, slice(0, cut), minus), (1, 1, slice(cut, LIST), plus)):
             far[k][i].wait_recv()
-            part[rel, rows] = (part[rel, rows].astype(F32) + far_in[i, rows].astype(F32)).astype(BF)
-            if k < STEPS - 1:
-                pl.semaphore_signal(far_free, 1, device_id=giver, device_id_type=MESH)
+            part[rel, rows, here] = (part[rel, rows, here].astype(F32) + far_in[i, rows, there].astype(F32)).astype(BF)
+            if k < STEPS - 2:
+                pl.semaphore_signal(far_free.at[k % 2], 1, device_id=giver, device_id_type=MESH)
             near[k][i].start()
 
     def send_back(k):
         part = all_part.at[k % 3]
+        near_in = all_near.at[k % 2]
         for copy in near[k]:
             copy.wait_recv()
         slot = k % 2
         if k >= 2:
             for copy in backs[k - 2]:
                 copy.wait_send()
-        for first in range(0, full, 1024):
+        if k in OVER_Z:
+            back[slot] = jnp.zeros(back.shape[1:], BF)
+            span = keep // 3
+            for first in range(0, keep, span):
+                there = pl.ds(pl.multiple_of(high * (full - keep) + first, LANES), span)
+                total = tn(picks[k], part[0, :, there]) + tn(picks[k], near_in[0, :, first : first + span])
+                total = total + tn(picks[k], near_in[1, :, first : first + span])
+                if first == 0:
+                    twice = (iota(total.shape, 1) < 2 * keep - full) & (high == 1)
+                    total = jnp.where(twice, 0.0, total)
+                back[slot, :, :, there] = total.astype(BF).reshape(BLOCKS, UNIT, span)
+        for first in range(0, 0 if k in OVER_Z else full, 1024):
             cols = slice(first, min(first + 1024, full))
             total = tn(picks[k], part[0, :, cols]) + tn(picks[k], near_in[0, :, cols])
             total = total + tn(picks[k], near_in[1, :, cols])
             back[slot, :, :, cols] = total.astype(BF).reshape(BLOCKS, UNIT, cols.stop - cols.start)
-        if k < STEPS - 1:
+        if k < STEPS - 2:
             for giver in (minus, plus):
-                pl.semaphore_signal(near_free, 1, device_id=giver, device_id_type=MESH)
+                pl.semaphore_signal(near_free.at[k % 2], 1, device_id=giver, device_id_type=MESH)
         me = core * 16 + y * 4 + z
         backs[k] = []
         for dz in range(4):
@@ -452,26 +508,28 @@
     share(1)
     forward(2)
     compute(1)
-    pass_on(0)
+    add_z(0)
     merge(1)
     share(2)
     forward(3)
     compute(2)
+    pass_on(0)
+    add_z(1)
+    merge(2)
+    share(3)
     send_back(0)
     pass_on(1)
-    merge(2)
-    share(3)
     compute(3)
     tell()
-    send_back(1)
     pass_on(2)
     merge(3)
-    gradients(0, 3)
+    send_back(1)
+    gradients(0, 2)
     send_back(2)
     pass_on(3)
-    gradients(3, 8)
+    gradients(2, 7)
     send_back(3)
-    gradients(8, 14)
+    gradients(7, 14)
 
     for dy, dz, dc in offsets[1:]:
         ay, az, ac = plane(dy, dz, dc)
@@ -497,7 +555,8 @@
     for copy in unit_copies + flag_copies + [parts[STEPS - 1]]:
         copy.wait_send()
     for k in range(STEPS):
-        for copy in own[k] + fwd[k] + twins[k]:
+        done = fwd[k] + twins[k][1:] if k < 2 else own[k] + fwd[k] + twins[k]
+        for copy in done:
             copy.wait_send()
     for k in range(STEPS - 3, STEPS):
         for copy in far[k] + near[k]:
@@ -510,6 +569,7 @@
     tokens, width = moe_input.shape
     hid = w_gate.shape[2]
     full = width // 2 + LANES
+    keep = (full // LANES + 1) // 2 * LANES
     vmem = pl.BlockSpec(memory_space=pltpu.VMEM)
     anywhere = pl.BlockSpec(memory_space=pl.ANY)
     dma = pltpu.SemaphoreType.DMA
@@ -535,14 +595,15 @@
             pltpu.VMEM((4, 2, 2, UNIT, width), BF),
             pltpu.VMEM((STEPS - 1, 2, 2, UNIT, width), BF),
             pltpu.VMEM((STEPS * BLOCKS, UNIT, width), BF),
-            pltpu.VMEM((STEPS, LIST, width + LANES), BF),
+            pltpu.VMEM((2, LIST, width + LANES), BF),
             pltpu.VMEM((2, 4, LIST, width + LANES), BF),
             pltpu.VMEM((STEPS, LIST, SLOTS), BF),
             pltpu.VMEM((3, 4, LIST, full), BF),
             pltpu.VMEM((4, LIST, full), BF),
             pltpu.VMEM((4, LIST, full), BF),
-            pltpu.VMEM((2, LIST, full), BF),
-            pltpu.VMEM((2, LIST, full), BF),
+            pltpu.VMEM((4, LIST, keep), BF),
+            pltpu.VMEM((2, 2, LIST, full), BF),
+            pltpu.VMEM((2, 2, LIST, full), BF),
             pltpu.VMEM((2, BLOCKS, UNIT, full), BF),
             pltpu.VMEM((PADDED, 3 * hid), F32),
             pltpu.VMEM((ROWS, 2 * hid), BF),
@@ -562,13 +623,16 @@
             dma((STEPS, 4)),
             dma((STEPS,)),
             dma((STEPS,)),
+            dma((STEPS,)),
+            dma((STEPS,)),
             dma((STEPS, 2)),
             dma((STEPS, 2)),
             dma((STEPS, 2)),
             dma((STEPS, 2)),
             regular,
             regular,
-            regular,
+            pltpu.SemaphoreType.REGULAR((2,)),
+            pltpu.SemaphoreType.REGULAR((2,)),
             dma((32,)),
             dma((32,)),
             dma((32,)),

time: 313 us -> 305 us (0.974)
  Pallas kernels: 297 us -> 290 us
    pallas_call x1, Pallas kernels: 297 us -> 290 us  [fast(): pl.pallas_call(kernel, out_shape=[jax.ShapeDtypeStruct((tokens, width), B...]
where the time goes in v4:
time: 305 us
  Pallas kernels  290 us (95%)
  local copies, waits for them, and re-layouts  13.1 us (4%)
    pallas_call x1, Pallas kernels, fast(): pl.pallas_call(kernel, out_shape=[jax.ShapeDtypeStruct((tokens, width), B...  290 us
    unnamed x15, local copies, waits for them, and re-layouts  11.9 us

profile of v4, /device:TPU:41, one launch (start us, length us, event | category | flops | bytes accessed | tf_op | source)
XLA Modules:
  0.0 304.6 jit_solution(1534360803948001655)
XLA Ops:
  0.6 0.0 copy-start.5
  0.6 0.0 copy-start.6
  0.7 0.0 copy-start.7
  0.7 289.9 %shard_map.112 = (bf16[36,7168]{1,0:T(8,128)(2,1)}, bf16[1,36]{1,0:T(2,128)(2,1)S(1)}, f32[8,128]{1,0:T(8,128)}, bf16[1,7168,256]{2,1,0:T(8,128)(2,1)}, bf16[1,7...) custom-call(bf16[36,7168]{1,0:T(8,128)(2,1)} %moe_input.1, ...), custom_call_target="tpu_custom_call" | custom-call | tf_op jit(solution)/shard_map/pallas_call | solution.py:577
  290.5 1.2 slice.3
  292.4 0.0 copy-done.5
  292.4 0.0 copy-done.6
  292.4 0.0 copy-done.7
  292.4 0.3 conditional.1
  292.7 1.9 copy.62
  294.6 0.5 copy.63
  295.1 0.0 copy-start.4
  295.1 4.3 %copy.64 = bf16[1,7168,256]{2,1,0:T(8,128)(2,1)} copy(bf16[1,7168,256]{2,1,0:T(8,128)(2,1)} %get-tuple-element.89) | data formatting | bytes 7340032
  299.4 0.0 copy-done.4
  299.4 0.0 copy-start.3
  299.4 1.9 copy.65
  301.2 1.5 copy-done.3
  302.7 1.8 copy.66
Async XLA Ops:
  0.6 291.7 %copy-start.5 = (bf16[36,7168]{1,0:T(8,128)(2,1)S(1)}, bf16[36,7168]{1,0:T(8,128)(2,1)}, u32[]{:S(2)}) copy-start(bf16[36,7168]{1,0:T(8,128)(2,1)} %out_grad.1) | copy-start | bytes 1548292
  0.6 291.7 %copy-start.6 = (s32[36,1]{0,1:T(1,128)S(1)}, s32[36,1]{0,1:T(1,128)}, u32[]{:S(2)}) copy-start(s32[36,1]{0,1:T(1,128)} %param.11) | copy-start | bytes 436
  0.7 291.7 %copy-start.7 = (bf16[36,1]{0,1:T(2,128)(2,1)S(1)}, bf16[36,1]{0,1:T(2,128)(2,1)}, u32[]{:S(2)}) copy-start(bf16[36,1]{0,1:T(2,128)(2,1)} %param.12) | copy-start | bytes 220
  295.1 4.3 %copy-start.4 = (bf16[1,7168,256]{2,1,0:T(8,128)(2,1)S(1)}, bf16[1,7168,256]{2,1,0:T(8,128)(2,1)}, u32[]{:S(2)}) copy-start(bf16[1,7168,256]{2,1,0:T(8,128)(2,1)} %get-tuple-element.90) | copy-start | bytes 11010052
  299.4 3.4 %copy-start.3 = (bf16[1,256,7168]{2,1,0:T(8,128)(2,1)S(1)}, bf16[1,256,7168]{2,1,0:T(8,128)(2,1)}, u32[]{:S(2)}) copy-start(bf16[1,256,7168]{2,1,0:T(8,128)(2,1)} %get-tuple-element.91) | copy-start | bytes 11010052

commit v5 on v4

--- a/solution.py
+++ b/solution.py
@@ -239,7 +239,7 @@
         copy.start()
         twins[k].append(copy)
 
-    def compute(k):
+    def compute(k, between=None):
         if k >= 2:
             kept[k].wait()
         for copy in twins[k]:
@@ -282,7 +282,8 @@
             wide = jnp.broadcast_to(piece, (LIST, LANES)).astype(BF)
             part[r, :, half:full] = wide
             twin_out[r, :, half:full] = wide
-        turned[k] = jnp.transpose(acc[...]).astype(BF)
+        if between is not None:
+            between()
         packed[...] = acc[0:ROWS, 0 : 2 * hid].astype(BF)
         span = 512
 
@@ -302,6 +303,7 @@
         parts[k] = remote(twin_out, twin_in, part_send.at[k], part_recv.at[k], device_id=twin)
         parts[k].start()
         rows_back(part, core * half)
+        turned[k] = jnp.transpose(acc[...]).astype(BF)
 
     def window(k):
         return (kept_cols, pl.ds(0, keep)) if k in OVER_Z else (pl.ds(0, full), pl.ds(0, full))
@@ -512,18 +514,17 @@
     merge(1)
     share(2)
     forward(3)
-    compute(2)
     pass_on(0)
     add_z(1)
+    compute(2)
     merge(2)
     share(3)
     send_back(0)
     pass_on(1)
-    compute(3)
-    tell()
-    pass_on(2)
+    compute(3, lambda: pass_on(2))
     merge(3)
     send_back(1)
+    tell()
     gradients(0, 2)
     send_back(2)
     pass_on(3)

time: 305 us -> 301 us (0.987); the launches traced: 305 us -> 297 us
  Pallas kernels: 290 us -> 282 us
    pallas_call x1, Pallas kernels: 290 us -> 282 us  [fast(): pl.pallas_call(kernel, out_shape=[jax.ShapeDtypeStruct((tokens, width), B...]
where the time goes in v5:
time: 301 us; the launch traced here: 297 us
  Pallas kernels  282 us (94%)
  local copies, waits for them, and re-layouts  13.1 us (4%)
    pallas_call x1, Pallas kernels, fast(): pl.pallas_call(kernel, out_shape=[jax.ShapeDtypeStruct((tokens, width), B...  282 us
    unnamed x15, local copies, waits for them, and re-layouts  11.9 us

profile of v5, /device:TPU:41, one launch (start us, length us, event | category | flops | bytes accessed | tf_op | source)
XLA Modules:
  0.0 297.0 jit_solution(3622662770698454418)
XLA Ops:
  0.6 0.0 copy-start.5
  0.6 0.0 copy-start.6
  0.7 0.0 copy-start.7
  0.7 282.3 %shard_map.112 = (bf16[36,7168]{1,0:T(8,128)(2,1)}, bf16[1,36]{1,0:T(2,128)(2,1)S(1)}, f32[8,128]{1,0:T(8,128)}, bf16[1,7168,256]{2,1,0:T(8,128)(2,1)}, bf16[1,7...) custom-call(bf16[36,7168]{1,0:T(8,128)(2,1)} %moe_input.1, ...), custom_call_target="tpu_custom_call" | custom-call | tf_op jit(solution)/shard_map/pallas_call | solution.py:578
  283.0 1.2 slice.3
  284.9 0.0 copy-done.5
  284.9 0.0 copy-done.6
  284.9 0.0 copy-done.7
  284.9 0.3 conditional.1
  285.2 1.9 copy.62
  287.1 0.5 copy.63
  287.6 0.0 copy-start.4
  287.6 4.3 %copy.64 = bf16[1,7168,256]{2,1,0:T(8,128)(2,1)} copy(bf16[1,7168,256]{2,1,0:T(8,128)(2,1)} %get-tuple-element.89) | data formatting | bytes 7340032
  291.8 0.0 copy-done.4
  291.8 0.0 copy-start.3
  291.8 1.9 copy.65
  293.7 1.5 copy-done.3
  295.2 1.8 copy.66
Async XLA Ops:
  0.6 284.2 %copy-start.5 = (bf16[36,7168]{1,0:T(8,128)(2,1)S(1)}, bf16[36,7168]{1,0:T(8,128)(2,1)}, u32[]{:S(2)}) copy-start(bf16[36,7168]{1,0:T(8,128)(2,1)} %out_grad.1) | copy-start | bytes 1548292
  0.6 284.2 %copy-start.6 = (s32[36,1]{0,1:T(1,128)S(1)}, s32[36,1]{0,1:T(1,128)}, u32[]{:S(2)}) copy-start(s32[36,1]{0,1:T(1,128)} %param.11) | copy-start | bytes 436
  0.7 284.2 %copy-start.7 = (bf16[36,1]{0,1:T(2,128)(2,1)S(1)}, bf16[36,1]{0,1:T(2,128)(2,1)}, u32[]{:S(2)}) copy-start(bf16[36,1]{0,1:T(2,128)(2,1)} %param.12) | copy-start | bytes 220
  287.6 4.3 %copy-start.4 = (bf16[1,7168,256]{2,1,0:T(8,128)(2,1)S(1)}, bf16[1,7168,256]{2,1,0:T(8,128)(2,1)}, u32[]{:S(2)}) copy-start(bf16[1,7168,256]{2,1,0:T(8,128)(2,1)} %get-tuple-element.90) | copy-start | bytes 11010052
  291.8 3.4 %copy-start.3 = (bf16[1,256,7168]{2,1,0:T(8,128)(2,1)S(1)}, bf16[1,256,7168]{2,1,0:T(8,128)(2,1)}, u32[]{:S(2)}) copy-start(bf16[1,256,7168]{2,1,0:T(8,128)(2,1)} %get-tuple-element.91) | copy-start | bytes 11010052
